TPU v7x, 128 devices: a whole 4x4x4 slice. The times are simulated.
128 devices in a mesh: ctx: 16 (over x_hi, z, core), head: 8 (over x_lo, y).
Axes of the slice: x: 4 (x_hi: 2, x_lo: 2; x = x_hi * 2 + x_lo), y: 4, z: 4, core: 2. Of those that a mesh axis runs over, the one named last changes fastest.
Arguments:
- coarse_query: bfloat16 [512, 3072], P(None, 'head'), may hold values from -5 to 5
- coarse_key: bfloat16 [512, 3072], P(None, 'head'), may hold values from -5 to 5
- coarse_value: bfloat16 [512, 3072], P(None, 'head'), may hold values from -5 to 5
- fine_query: bfloat16 [2048, 3072], P('ctx', 'head'), may hold values from -5 to 5
- fine_key: bfloat16 [2048, 3072], P('ctx', 'head'), may hold values from -5 to 5
- fine_value: bfloat16 [2048, 3072], P('ctx', 'head'), may hold values from -5 to 5
- coarse_sizes: int32 [6], replicated, may hold values from 1 to 128, 512 in all
- fine_sizes: int32 [6], replicated, may hold values from 1 to 512, 2048 in all
- fine_position: int32 [2048], P('ctx'), may hold values from 0 to 2047, as said below
- out_weight: bfloat16 [3072, 3072], P('head'), may hold values from -0.109375 to 0.109375
- coarse_cotangent: bfloat16 [512, 3072], P(None, 'head'), may hold values from -6 to 6
- fine_cotangent: bfloat16 [2048, 3072], P('ctx', 'head'), may hold values from -6 to 6
Outputs:
- coarse_out: bfloat16 [512, 3072], P(None, 'head')
- fine_out: bfloat16 [2048, 3072], P('ctx', 'head')
- coarse_dq: bfloat16 [512, 3072], P(None, 'head')
- coarse_dk: bfloat16 [512, 3072], P('ctx', 'head')
- coarse_dv: bfloat16 [512, 3072], P('ctx', 'head')
- fine_dq: bfloat16 [2048, 3072], P('ctx', 'head')
- fine_dk: bfloat16 [2048, 3072], P('ctx', 'head')
- fine_dv: bfloat16 [2048, 3072], P('ctx', 'head')
- out_weight_grad: float32 [3072, 3072], P('head', 'ctx')
Inputs may be any that keep to these rules, and one draw needn't show every extreme that they name: `coarse_sizes`: the sizes sum to 512. `fine_sizes`: the sizes sum to 2048. `fine_position`: a permutation of 0 .. 2047; every aligned run of 64 rows holds consecutive positions in rising order.
All inputs are finite; a program needn't handle non-finite values.
Results may differ from a plain program's by a relative error of at most 0.04.
Values may be sent and summed in bfloat16 or wider, within the bound.
A program may use at most 128 MiB of HBM per device.

v0:
```python
import math

import jax
import jax.numpy as jnp
from jax import lax
from jax.sharding import PartitionSpec as P

DH = 128


NEGATIVE = -1e30


def scale_ids(row_index, scale_sizes, first_scale):
    scale_ends = jnp.cumsum(scale_sizes)
    passed = (row_index[:, None] >= scale_ends[None, :]).astype(jnp.int32)
    return first_scale + jnp.sum(passed, axis=1)


def blocked(key_rows, value_rows, key_scale, block_width):
    block_count = key_rows.shape[0] // block_width
    head_count = key_rows.shape[1] // DH
    return (
        key_rows.reshape(block_count, block_width, head_count, DH),
        value_rows.reshape(block_count, block_width, head_count, DH),
        key_scale.reshape(block_count, block_width),
    )


def block_scores(query3, key_block, query_scale, key_scale):
    raw_scores = jnp.einsum(
        "qhd,khd->hqk", query3, key_block, preferred_element_type=jnp.float32
    ) * (1.0 / math.sqrt(DH))
    allowed = (key_scale[None, :] <= query_scale[:, None])[None]
    return (jnp.where(allowed, raw_scores, NEGATIVE), allowed)


def log_total(query3, key_groups, query_scale):

    def log_advance(running, key_piece):
        highest, totals = running
        key_block, value_block, key_scale = key_piece
        scores, allowed = block_scores(query3, key_block, query_scale, key_scale)
        new_high = jnp.maximum(highest, jnp.max(scores, axis=2))
        weights = jnp.where(allowed, jnp.exp(scores - new_high[:, :, None]), 0.0)
        return ((new_high, totals * jnp.exp(highest - new_high) + jnp.sum(weights, axis=2)), None)

    shape_rows = (query3.shape[1], query3.shape[0])
    running = (jnp.full(shape_rows, NEGATIVE, jnp.float32), jnp.zeros(shape_rows, jnp.float32))
    for key_group in key_groups:
        running, unused = lax.scan(log_advance, running, key_group)
    return running[0] + jnp.log(running[1])


def attend(query3, key_groups, query_scale, log_sums):

    def attend_advance(accumulated, key_piece):
        key_block, value_block, key_scale = key_piece
        scores, allowed = block_scores(query3, key_block, query_scale, key_scale)
        weights = jnp.where(allowed, jnp.exp(scores - log_sums[:, :, None]), 0.0).astype(
            jnp.bfloat16
        )
        return (
            accumulated
            + jnp.einsum("hqk,khd->qhd", weights, value_block, preferred_element_type=jnp.float32),
            None,
        )

    accumulated = jnp.zeros(query3.shape, jnp.float32)
    for key_group in key_groups:
        accumulated, unused = lax.scan(attend_advance, accumulated, key_group)
    return accumulated.reshape(query3.shape[0], -1).astype(jnp.bfloat16)


def row_deltas(grad_rows, attn_rows, head_count):
    product = grad_rows.astype(jnp.float32) * attn_rows.astype(jnp.float32)
    return jnp.sum(product.reshape(product.shape[0], head_count, DH), axis=2).T


def backward(query3, grad_heads, query_scale, log_sums, deltas, key_group):
    factor = 1.0 / math.sqrt(DH)

    def backward_advance(grad_query, key_piece):
        key_block, value_block, key_scale = key_piece
        scores, allowed = block_scores(query3, key_block, query_scale, key_scale)
        unrounded = jnp.where(allowed, jnp.exp(scores - log_sums[:, :, None]), 0.0)
        grad_probs = jnp.einsum(
            "qhd,khd->hqk", grad_heads, value_block, preferred_element_type=jnp.float32
        )
        grad_scores = (unrounded * (grad_probs - deltas[:, :, None]) * factor).astype(jnp.bfloat16)
        grad_query = grad_query + jnp.einsum(
            "hqk,khd->qhd", grad_scores, key_block, preferred_element_type=jnp.float32
        )
        grad_key = jnp.einsum(
            "hqk,qhd->khd", grad_scores, query3, preferred_element_type=jnp.float32
        )
        grad_value = jnp.einsum(
            "hqk,qhd->khd",
            unrounded.astype(jnp.bfloat16),
            grad_heads,
            preferred_element_type=jnp.float32,
        )
        return (grad_query, (grad_key, grad_value))

    grad_query, stacked = lax.scan(
        backward_advance, jnp.zeros(query3.shape, jnp.float32), key_group
    )
    key_total = key_group[0].shape[0] * key_group[0].shape[1]
    return (grad_query, stacked[0].reshape(key_total, -1), stacked[1].reshape(key_total, -1))


def on_device(
    coarse_query,
    coarse_key,
    coarse_value,
    fine_query,
    fine_key,
    fine_value,
    coarse_sizes,
    fine_sizes,
    fine_position,
    out_weight,
    coarse_cotangent,
    fine_cotangent,
):
    ctx_count = lax.axis_size("ctx")
    ctx_index = lax.axis_index("ctx")
    coarse_count = coarse_query.shape[0]
    fine_count = fine_query.shape[0]
    heads_local = coarse_query.shape[1] // DH
    coarse_scales = coarse_sizes.shape[0]
    share_rows = coarse_count // ctx_count
    share_start = ctx_index * share_rows
    block_width = min(512, coarse_count)
    coarse_scale = scale_ids(jnp.arange(coarse_count, dtype=jnp.int32), coarse_sizes, 0)
    fine_scale = scale_ids(fine_position, fine_sizes, coarse_scales)
    all_keys, all_values, all_positions = (
        lax.all_gather(fine_key, "ctx", axis=0, tiled=True),
        lax.all_gather(fine_value, "ctx", axis=0, tiled=True),
        lax.all_gather(fine_position, "ctx", axis=0, tiled=True),
    )
    coarse_group = blocked(coarse_key, coarse_value, coarse_scale, block_width)
    fine_group = blocked(
        all_keys, all_values, scale_ids(all_positions, fine_sizes, coarse_scales), block_width
    )
    query_count = coarse_query.shape[0]
    query3 = coarse_query.reshape(query_count, heads_local, DH)
    coarse_log = log_total(query3, [coarse_group], coarse_scale)
    coarse_attn = attend(query3, [coarse_group], coarse_scale, coarse_log)
    fine_query3 = fine_query.reshape(fine_count, heads_local, DH)
    fine_log = log_total(fine_query3, [coarse_group, fine_group], fine_scale)
    fine_attn = attend(fine_query3, [coarse_group, fine_group], fine_scale, fine_log)
    coarse_term = jnp.dot(coarse_attn, out_weight, preferred_element_type=jnp.float32)
    fine_term = jnp.dot(fine_attn, out_weight, preferred_element_type=jnp.float32)
    coarse_sum, fine_sum = (
        lax.psum_scatter(coarse_term, "head", scatter_dimension=1, tiled=True),
        lax.psum_scatter(fine_term, "head", scatter_dimension=1, tiled=True),
    )
    coarse_out_rows = coarse_sum.astype(jnp.bfloat16)
    fine_out = fine_sum.astype(jnp.bfloat16)
    share_attn = lax.dynamic_slice_in_dim(coarse_attn, share_start, share_rows, 0)
    weight_attn = jnp.concatenate([fine_attn, share_attn], axis=0)
    coarse_piece = lax.all_gather(coarse_cotangent, "head", axis=1, tiled=True)
    fine_piece = lax.all_gather(fine_cotangent, "head", axis=1, tiled=True)
    contract_last = (((1,), (1,)), ((), ()))
    coarse_grad = lax.dot_general(
        coarse_piece, out_weight, contract_last, preferred_element_type=jnp.float32
    )
    fine_grad = lax.dot_general(
        fine_piece, out_weight, contract_last, preferred_element_type=jnp.float32
    )
    share_piece = lax.dynamic_slice_in_dim(coarse_piece, share_start, share_rows, 0)
    stacked_piece = jnp.concatenate([fine_piece, share_piece], axis=0)
    update = lax.dot_general(
        weight_attn, stacked_piece, (((0,), (0,)), ((), ())), preferred_element_type=jnp.float32
    )
    weight_grad = update
    coarse_grad, fine_grad, weight_grad = (coarse_grad, fine_grad, weight_grad)
    coarse_grad = coarse_grad.astype(jnp.bfloat16)
    fine_grad = fine_grad.astype(jnp.bfloat16)
    coarse_delta = row_deltas(coarse_grad, coarse_attn, heads_local)
    fine_delta = row_deltas(fine_grad, fine_attn, heads_local)
    coarse_grad3 = coarse_grad.reshape(query_count, heads_local, DH)
    fine_grad3 = fine_grad.reshape(fine_count, heads_local, DH)
    coarse_dq_rows, coarse_keys_own, coarse_values_own = backward(
        query3, coarse_grad3, coarse_scale, coarse_log, coarse_delta, coarse_group
    )
    fine_dq_near, fine_coarse_keys, fine_coarse_values = backward(
        fine_query3, fine_grad3, fine_scale, fine_log, fine_delta, coarse_group
    )
    fine_dq_far, fine_key_term, fine_value_term = backward(
        fine_query3, fine_grad3, fine_scale, fine_log, fine_delta, fine_group
    )
    weight_part, coarse_key_part, coarse_value_part, fine_key_part, fine_value_part = (
        lax.psum_scatter(weight_grad, "ctx", scatter_dimension=1, tiled=True),
        lax.psum_scatter(fine_coarse_keys, "ctx", scatter_dimension=0, tiled=True),
        lax.psum_scatter(fine_coarse_values, "ctx", scatter_dimension=0, tiled=True),
        lax.psum_scatter(fine_key_term, "ctx", scatter_dimension=0, tiled=True),
        lax.psum_scatter(fine_value_term, "ctx", scatter_dimension=0, tiled=True),
    )
    fine_dk = fine_key_part.astype(jnp.bfloat16)
    fine_dv = fine_value_part.astype(jnp.bfloat16)
    fine_dq = (fine_dq_near + fine_dq_far).reshape(fine_count, -1).astype(jnp.bfloat16)
    coarse_dq_local = coarse_dq_rows.reshape(query_count, -1).astype(jnp.bfloat16)
    coarse_dk = (
        coarse_key_part + lax.dynamic_slice_in_dim(coarse_keys_own, share_start, share_rows, 0)
    ).astype(jnp.bfloat16)
    coarse_dv = (
        coarse_value_part + lax.dynamic_slice_in_dim(coarse_values_own, share_start, share_rows, 0)
    ).astype(jnp.bfloat16)
    return (
        coarse_out_rows,
        fine_out,
        coarse_dq_local,
        coarse_dk,
        coarse_dv,
        fine_dq,
        fine_dk,
        fine_dv,
        weight_part,
    )


def solution(mesh):
    placed = (
        P(None, "head"),
        P(None, "head"),
        P(None, "head"),
        P("ctx", "head"),
        P("ctx", "head"),
        P("ctx", "head"),
        P(),
        P(),
        P("ctx"),
        P("head", None),
        P(None, "head"),
        P("ctx", "head"),
    )
    return jax.shard_map(
        on_device,
        mesh=mesh,
        in_specs=placed,
        out_specs=(
            P(None, "head"),
            P("ctx", "head"),
            P(None, "head"),
            P("ctx", "head"),
            P("ctx", "head"),
            P("ctx", "head"),
            P("ctx", "head"),
            P("ctx", "head"),
            P("head", "ctx"),
        ),
        check_vma=False,
    )
```

profile of v0, /device:TPU:1, one launch (start us, length us, event | category | flops | bytes accessed | tf_op | source)
XLA Modules:
  0.0 663.7 jit_solution(11941830806177057585)
XLA Ops:
  16.9 26.6 %all-gather = s32[16,1,128]{2,1,0:T(1,128)S(1)} all-gather(s32[1,1,128]{2,1,0:T(1,128)S(1)} %bitcast.260), channel_id=1, replica_groups=mesh['ctx'=16,'head'=8] {'ctx'}, dimensions={0}, use_global_device_ids=true | all-gather | bytes 8704 | tf_op jit(solution)/shard_map/all_gather | solution.py:140
  45.6 27.8 %all_gather.19 = bf16[128,3072]{1,0:T(8,128)(2,1)} all-gather(bf16[128,384]{1,0:T(8,128)(2,1)} %param.29), channel_id=1, replica_groups=mesh['ctx'=16,'head'=8] {'head'}, dimensions={1}, use_global_device_ids=true | all-gather | bytes 884736 | tf_op jit(solution)/shard_map/all_gather | solution.py:164
  73.4 5.1 reshape.315
  78.5 3.1 copy.161
  81.6 6.7 %while.7 = (s32[]{:T(128)}, f32[3,128]{1,0:T(4,128)S(1)}, f32[3,128]{1,0:T(4,128)S(1)}, s32[4,512]{1,0:T(4,128)S(1)}, s32[128]{0:T(128)S(1)}, /*index=5*/bf16[4,...) while((s32[]{:T(128)}, f32[3,128]{1,0:T(4,128)S(1)}, f32[3,128]{1,0:T(4,128)S(1)}, ...), condition=%wide.region_13.14_spmd, body=%wide.region_10.13_spmd.sunk | while | flops 51577600 | bytes 2288217 | solution.py:51
  92.6 16.1 %all-gather.7.cloned.1.call-done = bf16[2048,384]{1,0:T(8,128)(2,1)} async-done(((bf16[128,384]{1,0:T(8,128)(2,1)}), bf16[2048,384]{1,0:T(8,128)(2,1)}) %all-gather.7.cloned.1.call-update) | async-done | bytes 1572880 | tf_op jit(solution)/shard_map/all_gather | solution.py:139
  111.4 3.9 reshape.302
  118.2 10.3 %while.8 = (s32[]{:T(128)}, f32[128,3,128]{0,2,1:T(8,128)}, bf16[4,512,3,128]{1,3,2,0:T(8,128)(2,1)}, s32[4,512]{1,0:T(4,128)S(1)}, s32[128]{0:T(128)S(1)}, /*in...) while((s32[]{:T(128)}, f32[128,3,128]{0,2,1:T(8,128)}, ...), condition=%wide.region_15.16_spmd, body=%wide.region_14.15_spmd.sunk | while | flops 101761024 | bytes 1418849 | solution.py:71
  148.8 3.9 copy.186
  154.7 185.8 %while.9 = (s32[]{:T(128)}, f32[128,3,128]{0,2,1:T(8,128)}, f32[4,512,3,128]{1,0,3,2:T(4,128)}, f32[4,512,3,128]{1,0,3,2:T(4,128)}, bf16[4,512,3,128]{3,1,2,0:T(...) while((s32[]{:T(128)}, f32[128,3,128]{0,2,1:T(8,128)}, ...), condition=%wide.region_22.23_spmd.clone, body=%wide.region_21.22_spmd.clone.sunk | while | flops 253591552 | bytes 14298835 | solution.py:105
  159.6 3.0 copy.227
  162.6 16.2 %dynamic_update_slice.20 = f32[4,512,3,128]{1,0,3,2:T(4,128)} dynamic-update-slice(f32[4,512,3,128]{1,0,3,2:T(4,128)} %get-tuple-element.797, f32[1,512,3,128]{1,0,3,2:T(1,128)} %copy.227, s32[]{:T(128)} %get-tuple-element.795, s32[]{:T(128)} %constant.158.clone.1..sunk, s32[]{:T(128)} %constant.158.clone.1..sunk, s32[]{:T(128)} %constant.158.clone.1..sunk) | dynamic-update-slice | bytes 1572868 | tf_op jit(solution)/shard_map/while/body/jit(dynamic_update_index_in_dim)/dynamic_update_slice | solution.py:105
  185.1 16.1 %dynamic_update_slice.21 = f32[4,512,3,128]{1,0,3,2:T(4,128)} dynamic-update-slice(f32[4,512,3,128]{1,0,3,2:T(4,128)} %get-tuple-element.798, f32[1,512,3,128]{1,0,3,2:T(1,128)S(1)} %copy.228, s32[]{:T(128)} %get-tuple-element.795, s32[]{:T(128)} %constant.158.clone.1..sunk, s32[]{:T(128)} %constant.158.clone.1..sunk, s32[]{:T(128)} %constant.158.clone.1..sunk) | dynamic-update-slice | bytes 1572868 | tf_op jit(solution)/shard_map/while/body/jit(dynamic_update_index_in_dim)/dynamic_update_slice | solution.py:105
  206.0 3.0 copy.227
  209.0 16.1 %dynamic_update_slice.20 = f32[4,512,3,128]{1,0,3,2:T(4,128)} dynamic-update-slice(f32[4,512,3,128]{1,0,3,2:T(4,128)} %get-tuple-element.797, f32[1,512,3,128]{1,0,3,2:T(1,128)} %copy.227, s32[]{:T(128)} %get-tuple-element.795, s32[]{:T(128)} %constant.158.clone.1..sunk, s32[]{:T(128)} %constant.158.clone.1..sunk, s32[]{:T(128)} %constant.158.clone.1..sunk) | dynamic-update-slice | bytes 1572868 | tf_op jit(solution)/shard_map/while/body/jit(dynamic_update_index_in_dim)/dynamic_update_slice | solution.py:105
  231.5 16.1 %dynamic_update_slice.21 = f32[4,512,3,128]{1,0,3,2:T(4,128)} dynamic-update-slice(f32[4,512,3,128]{1,0,3,2:T(4,128)} %get-tuple-element.798, f32[1,512,3,128]{1,0,3,2:T(1,128)S(1)} %copy.228, s32[]{:T(128)} %get-tuple-element.795, s32[]{:T(128)} %constant.158.clone.1..sunk, s32[]{:T(128)} %constant.158.clone.1..sunk, s32[]{:T(128)} %constant.158.clone.1..sunk) | dynamic-update-slice | bytes 1572868 | tf_op jit(solution)/shard_map/while/body/jit(dynamic_update_index_in_dim)/dynamic_update_slice | solution.py:105
  252.5 3.0 copy.227
  255.5 16.1 %dynamic_update_slice.20 = f32[4,512,3,128]{1,0,3,2:T(4,128)} dynamic-update-slice(f32[4,512,3,128]{1,0,3,2:T(4,128)} %get-tuple-element.797, f32[1,512,3,128]{1,0,3,2:T(1,128)} %copy.227, s32[]{:T(128)} %get-tuple-element.795, s32[]{:T(128)} %constant.158.clone.1..sunk, s32[]{:T(128)} %constant.158.clone.1..sunk, s32[]{:T(128)} %constant.158.clone.1..sunk) | dynamic-update-slice | bytes 1572868 | tf_op jit(solution)/shard_map/while/body/jit(dynamic_update_index_in_dim)/dynamic_update_slice | solution.py:105
  278.0 16.1 %dynamic_update_slice.21 = f32[4,512,3,128]{1,0,3,2:T(4,128)} dynamic-update-slice(f32[4,512,3,128]{1,0,3,2:T(4,128)} %get-tuple-element.798, f32[1,512,3,128]{1,0,3,2:T(1,128)S(1)} %copy.228, s32[]{:T(128)} %get-tuple-element.795, s32[]{:T(128)} %constant.158.clone.1..sunk, s32[]{:T(128)} %constant.158.clone.1..sunk, s32[]{:T(128)} %constant.158.clone.1..sunk) | dynamic-update-slice | bytes 1572868 | tf_op jit(solution)/shard_map/while/body/jit(dynamic_update_index_in_dim)/dynamic_update_slice | solution.py:105
  298.9 3.0 copy.227
  301.9 16.1 %dynamic_update_slice.20 = f32[4,512,3,128]{1,0,3,2:T(4,128)} dynamic-update-slice(f32[4,512,3,128]{1,0,3,2:T(4,128)} %get-tuple-element.797, f32[1,512,3,128]{1,0,3,2:T(1,128)} %copy.227, s32[]{:T(128)} %get-tuple-element.795, s32[]{:T(128)} %constant.158.clone.1..sunk, s32[]{:T(128)} %constant.158.clone.1..sunk, s32[]{:T(128)} %constant.158.clone.1..sunk) | dynamic-update-slice | bytes 1572868 | tf_op jit(solution)/shard_map/while/body/jit(dynamic_update_index_in_dim)/dynamic_update_slice | solution.py:105
  324.4 16.1 %dynamic_update_slice.21 = f32[4,512,3,128]{1,0,3,2:T(4,128)} dynamic-update-slice(f32[4,512,3,128]{1,0,3,2:T(4,128)} %get-tuple-element.798, f32[1,512,3,128]{1,0,3,2:T(1,128)S(1)} %copy.228, s32[]{:T(128)} %get-tuple-element.795, s32[]{:T(128)} %constant.158.clone.1..sunk, s32[]{:T(128)} %constant.158.clone.1..sunk, s32[]{:T(128)} %constant.158.clone.1..sunk) | dynamic-update-slice | bytes 1572868 | tf_op jit(solution)/shard_map/while/body/jit(dynamic_update_index_in_dim)/dynamic_update_slice | solution.py:105
  340.5 4.9 copy.223
  345.5 4.9 copy.224
  355.3 4.5 fusion.77
  362.7 4.3 fusion.58
  369.1 4.4 convert_multiply_fusion
  378.1 3.4 multiply_convert_fusion
  390.6 27.6 %reduce-scatter.16.cloned.1.call-done = f32[128,384]{0,1:T(8,128)} async-done(((f32[2048,384]{0,1:T(8,128)}), f32[128,384]{0,1:T(8,128)}) %reduce-scatter.16.cloned.1.call-update) | async-done | bytes 196624 | tf_op jit(solution)/shard_map/reduce_scatter | solution.py:198
  419.9 76.6 %reduce-scatter.18.cloned.1.call-done = f32[128,384]{0,1:T(8,128)} async-done(((f32[2048,384]{0,1:T(8,128)}), f32[128,384]{0,1:T(8,128)}) %reduce-scatter.18.cloned.1.call-update) | async-done | bytes 196624 | tf_op jit(solution)/shard_map/reduce_scatter | solution.py:199
  498.3 73.6 %reduce-scatter.8.cloned.1.call-done = f32[512,384]{1,0:T(8,128)} async-done(((f32[512,3072]{1,0:T(8,128)}), f32[512,384]{1,0:T(8,128)}) %reduce-scatter.8.cloned.1.call-update) | async-done | bytes 786448 | tf_op jit(solution)/shard_map/reduce_scatter | solution.py:156
  573.8 83.1 %reduce-scatter.20.cloned.1.call-done = f32[384,192]{0,1:T(8,128)} async-done(((f32[384,3072]{0,1:T(8,128)}), f32[384,192]{0,1:T(8,128)}) %reduce-scatter.20.cloned.1.call-update) | async-done | bytes 294928 | tf_op jit(solution)/shard_map/reduce_scatter | solution.py:195
  (223 shorter events, 133.9 us)
Async XLA Ops:
  7.2 124.6 %copy-start = (bf16[384,3072]{1,0:T(8,128)(2,1)S(1)}, bf16[384,3072]{1,0:T(8,128)(2,1)}, u32[]{:S(2)}) copy-start(bf16[384,3072]{1,0:T(8,128)(2,1)} %param.27) | copy-start | bytes 7077892
  7.2 9.7 %copy-start.22 = (s32[128]{0:T(128)S(1)}, s32[128]{0:T(128)}, u32[]{:S(2)}) copy-start(s32[128]{0:T(128)} %param.26) | copy-start | bytes 1540
  7.2 66.2 %all-gather.5.cloned.1.call-start = ((), (), s32[]{:S(2)}) async-start(), calls=%async_computation.8 | async-start | bytes 1671168 | tf_op jit(solution)/shard_map/all_gather | solution.py:138
  7.9 100.8 %all-gather.7.cloned.1.call-start = ((), (), s32[]{:S(2)}) async-start(), calls=%async_computation.9 | async-start | bytes 1671168 | tf_op jit(solution)/shard_map/all_gather | solution.py:139
  8.7 353.1 %all-gather.9.cloned.1.call-start = ((), (), s32[]{:S(2)}) async-start(), calls=%async_computation.11 | async-start | bytes 3538944 | tf_op jit(solution)/shard_map/all_gather | solution.py:163
  9.4 376.8 %reduce-scatter.14.cloned.1.call-start = ((), (), s32[]{:S(2)}) async-start(), calls=%async_computation.13 | async-start | bytes 835584 | tf_op jit(solution)/shard_map/reduce_scatter | solution.py:197
  12.0 66.5 %copy-start.20 = (s32[512]{0:T(512)}, s32[512]{0:T(512)S(1)}, u32[]{:S(2)}) copy-start(s32[512]{0:T(512)S(1)} %convert_reduce_fusion.1) | copy-start | bytes 6148
  140.7 247.0 %reduce-scatter.12.cloned.1.call-start = ((), (), s32[]{:S(2)}) async-start(), calls=%async_computation.12 | async-start | bytes 835584 | tf_op jit(solution)/shard_map/reduce_scatter | solution.py:196
  145.9 6.8 %copy-start.17 = (bf16[128,3,128]{0,2,1:T(8,128)(2,1)S(1)}, bf16[128,3,128]{0,2,1:T(8,128)(2,1)}, u32[]{:S(2)}) copy-start(bf16[128,3,128]{0,2,1:T(8,128)(2,1)} %convert_element_type.113) | copy-start | bytes 294916
  147.1 242.0 %reduce-scatter.10.cloned.1.call-start = ((), (), s32[]{:S(2)}) async-start(), calls=%async_computation.10 | async-start | bytes 1769472 | tf_op jit(solution)/shard_map/reduce_scatter | solution.py:157
  154.5 263.8 %reduce-scatter.16.cloned.1.call-start = ((), (), s32[]{:S(2)}) async-start(), calls=%async_computation.14 | async-start | bytes 3342336 | tf_op jit(solution)/shard_map/reduce_scatter | solution.py:198
  154.7 1.5 copy-start.3
  180.8 20.4 %copy-start.4 = (bf16[128,3,128]{2,0,1:T(8,128)(2,1)S(1)}, bf16[128,3,128]{2,0,1:T(8,128)(2,1)}, u32[]{:S(2)}) copy-start(bf16[128,3,128]{2,0,1:T(8,128)(2,1)} %copy-done.3) | copy-start | bytes 294916 | tf_op jit(solution)/shard_map/while
  201.1 1.5 copy-start.3
  227.2 20.4 %copy-start.4 = (bf16[128,3,128]{2,0,1:T(8,128)(2,1)S(1)}, bf16[128,3,128]{2,0,1:T(8,128)(2,1)}, u32[]{:S(2)}) copy-start(bf16[128,3,128]{2,0,1:T(8,128)(2,1)} %copy-done.3) | copy-start | bytes 294916 | tf_op jit(solution)/shard_map/while
  247.6 1.5 copy-start.3
  273.7 20.3 %copy-start.4 = (bf16[128,3,128]{2,0,1:T(8,128)(2,1)S(1)}, bf16[128,3,128]{2,0,1:T(8,128)(2,1)}, u32[]{:S(2)}) copy-start(bf16[128,3,128]{2,0,1:T(8,128)(2,1)} %copy-done.3) | copy-start | bytes 294916 | tf_op jit(solution)/shard_map/while
  294.0 1.5 copy-start.3
  320.1 20.3 %copy-start.4 = (bf16[128,3,128]{2,0,1:T(8,128)(2,1)S(1)}, bf16[128,3,128]{2,0,1:T(8,128)(2,1)}, u32[]{:S(2)}) copy-start(bf16[128,3,128]{2,0,1:T(8,128)(2,1)} %copy-done.3) | copy-start | bytes 294916 | tf_op jit(solution)/shard_map/while
  345.4 151.2 %reduce-scatter.18.cloned.1.call-start = ((), (), s32[]{:S(2)}) async-start(), calls=%async_computation.15 | async-start | bytes 3342336 | tf_op jit(solution)/shard_map/reduce_scatter | solution.py:199
  350.4 1.4 copy-start.5
  350.4 221.4 %reduce-scatter.8.cloned.1.call-start = ((), (), s32[]{:S(2)}) async-start(), calls=%async_computation.7 | async-start | bytes 7077888 | tf_op jit(solution)/shard_map/reduce_scatter | solution.py:156
  351.6 1.9 copy-start.9
  351.8 1.7 copy-start.11
  351.9 1.7 copy-start.13
  352.7 1.9 copy-start.1
  359.8 2.9 copy-start.6
  359.9 297.1 %reduce-scatter.20.cloned.1.call-start = ((), (), s32[]{:S(2)}) async-start(), calls=%async_computation.16 | async-start | bytes 5013504 | tf_op jit(solution)/shard_map/reduce_scatter | solution.py:195
  369.1 4.4 copy-start.2
  369.1 4.4 copy-start.12
  373.6 4.5 copy-start.14
  378.1 4.6 copy-start.10
  (8 other events, 8.1 us)
Sparse Core Ops, SparseCore 0:
  10.5 50.9 all-gather.4
  64.0 44.7 all-gather.6
  110.4 39.8 all-gather.8
  153.9 66.4 reduce-scatter.13
  224.5 65.1 reduce-scatter.11
  292.0 36.6 reduce-scatter.9
  345.5 72.6 reduce-scatter.15
  422.3 74.2 reduce-scatter.17
  499.0 72.8 reduce-scatter.7
  576.4 80.4 reduce-scatter.19
where the time goes:
time: 670 us; the launch traced here: 664 us
  waiting for transfers between devices  279 us (42%)
  local copies, waits for them, and re-layouts  211 us (31%)
  matrix products  84.1 us (13%)
  blocking collectives  54.4 us (8%)
  other arithmetic  19.2 us (3%)
  between operations  14.6 us (2%)
    dynamic_update_slice x16, local copies, waits for them, and re-layouts, backward(): lax.scan(backward_advance, jnp.zeros(query3.shape, jnp.float32), key_group)  150 us
    reduce_scatter x1, waiting for transfers between devices, on_device(): lax.psum_scatter(weight_grad, 'ctx', scatter_dimension=1, tiled=True)  83.1 us
    reduce_scatter x1, waiting for transfers between devices, on_device(): lax.psum_scatter(fine_value_term, 'ctx', scatter_dimension=0, tiled=True)  76.6 us
    reduce_scatter x1, waiting for transfers between devices, on_device(): lax.psum_scatter(coarse_term, 'head', scatter_dimension=1, tiled=True)  73.6 us
    unnamed x58, local copies, waits for them, and re-layouts  29.4 us
    all_gather x1, blocking collectives, on_device(): fine_piece = lax.all_gather(fine_cotangent, 'head', axis=1, tiled=True)  27.8 us
    reduce_scatter x1, waiting for transfers between devices, on_device(): lax.psum_scatter(fine_key_term, 'ctx', scatter_dimension=0, tiled=True)  27.6 us
    all_gather x1, blocking collectives, on_device(): lax.all_gather(fine_position, 'ctx', axis=0, tiled=True)  26.6 us
  transfers between devices with their start and end apart: 10, of which 5 were waited for; matrix products, arithmetic and copies ran while one was open for 47% of the time, Pallas kernels for 0%

commit v1 on v0

v1 whole, which is shorter than its diff:
```python
import math

import jax
import jax.numpy as jnp
from jax import lax
from jax.experimental import pallas as pl
from jax.experimental.pallas import tpu as pltpu
from jax.sharding import PartitionSpec as P

DH = 128
HL = 3
FR = 128
CR = 32
R = FR + CR
KR = 272
CH = 512
NEG = -1e30
BF = jnp.bfloat16
F32 = jnp.float32
MESH = pl.DeviceIdType.MESH
NT = (((1,), (1,)), ((), ()))
TN = (((0,), (0,)), ((), ()))
NN = (((1,), (0,)), ((), ()))


def dot(a, b, dims):
    return lax.dot_general(a, b, dims, preferred_element_type=F32)


def ctx_of(slot):
    core, rest = divmod(slot, 8)
    z, xh = divmod(rest, 2)
    return (xh * 4 + z) * 2 + core


def kernel(
    cq, ck, cv, fq, fk, fv, csz, fsz, fpos, w, cc, fc,
    cout, fout, cdq, cdk, cdv, fdq, fdk, fdv, wg,
    qs, kv, cotb, ksc, tbuf, ebuf, attn_s, do_s,
    part, sibr, ra, rb, r1, r3, rx,
    opart, ora, orb, or1, or3, orx, fbuf, wsend, wrecv,
    ssem, rsem,
):
    ctx = lax.axis_index("ctx")
    head = lax.axis_index("head")
    core = ctx % 2
    z = (ctx // 2) % 4
    xh = ctx // 8
    y = head % 4
    xl = head // 4
    z1 = z + 1 - 2 * (z % 2)
    z3 = 3 - z
    z2 = (z + 2) % 4
    y1 = y + 1 - 2 * (y % 2)
    y3 = 3 - y
    y2 = (y + 2) % 4

    def ctx_id(a, b, c):
        return ((a * 4 + b) * 2 + c, head)

    sib = ctx_id(xh, z, 1 - core)
    px = ctx_id(1 - xh, z, core)
    pz1 = ctx_id(xh, z1, core)
    pz3 = ctx_id(xh, z3, core)
    py1 = (ctx, xl * 4 + y1)
    py3 = (ctx, xl * 4 + y3)
    pxl = (ctx, (1 - xl) * 4 + y)
    peers = (sib, px, pz1, pz3, py1, py3, pxl)

    count = [0]
    started = []

    def send(src, dst, peer):
        i = count[0]
        count[0] += 1
        copy = pltpu.make_async_remote_copy(
            src_ref=src,
            dst_ref=dst,
            send_sem=ssem.at[i],
            recv_sem=rsem.at[i],
            device_id=peer,
            device_id_type=MESH,
        )
        copy.start()
        started.append(copy)
        return copy

    iota_l = lax.broadcasted_iota(jnp.int32, (1, 128), 1)

    def scale_of(position, sizes, first):
        end = jnp.int32(0)
        total = jnp.zeros(position.shape, jnp.int32) + first
        for s in range(6):
            end = end + sizes[s]
            total = total + (position >= end).astype(jnp.int32)
        return total.astype(F32)

    fsc_row = scale_of(fpos[...], fsz, 6)
    own = core * 8 + z * 2 + xh
    for h in range(HL):
        hs = pl.ds(h * DH, DH)
        kv[h, own, 0:128, :] = fk[:, hs]
        kv[h, own, 128:256, :] = fv[:, hs]
        kv[h, own, 256:272, :] = jnp.broadcast_to(fsc_row, (16, 128)).astype(BF)
    cotb[y * 2 + xl, 0:FR, :] = fc[...]
    cotb[y * 2 + xl, FR:R, :] = cc[pl.ds(pl.multiple_of(ctx * CR, CR), CR), :]

    barrier = pltpu.get_barrier_semaphore()
    for peer in peers:
        pl.semaphore_signal(barrier, inc=1, device_id=peer, device_id_type=MESH)
    pl.semaphore_wait(barrier, len(peers))

    class Gather:
        def __init__(self, at, split, pair, ring, ring1, ring3, first, ids, sibling):
            self.at, self.split = at, split
            self.pair, self.ring, self.ring1, self.ring3, self.first = pair, ring, ring1, ring3, first
            self.ids, self.sibling = ids, sibling

        def a(self):
            v = self.at(self.first + self.ring * 2 + self.pair, 1, None)
            self.cx = send(v, v, self.ids[0])

        def b(self):
            self.cx.wait_recv()
            v = self.at(self.first + self.ring * 2, 2, None)
            self.c1 = send(v, v, self.ids[1])
            self.c3 = send(v, v, self.ids[2])

        def c(self):
            self.c1.wait_recv()
            v = self.at(self.first + self.ring1 * 2, 2, 0)
            self.ca = send(v, v, self.ids[2])
            self.c3.wait_recv()
            v = self.at(self.first + self.ring3 * 2, 2, 1)
            self.cb = send(v, v, self.ids[1])

        def d(self):
            self.ca.wait_recv()
            self.cb.wait_recv()
            if self.sibling is not None:
                v = self.at(self.first, 8, None)
                self.cs = send(v, v, self.sibling)

        def e(self):
            if self.sibling is not None:
                self.cs.wait_recv()

    ctx_ids = (px, pz1, pz3)
    head_ids = (pxl, py1, py3)

    def rows_at(ref, cut, total):
        def at(slot, n, half):
            if half is None:
                return ref.at[pl.ds(slot, n)]
            return ref.at[pl.ds(slot, n), pl.ds(0, cut) if half == 0 else pl.ds(cut, total - cut)]

        return at

    gathers = [
        Gather(rows_at(kv.at[h], 128, KR), None, xh, z, z1, z3, core * 8, ctx_ids, sib)
        for h in range(HL)
    ]
    cot_gather = Gather(rows_at(cotb, 80, R), None, xl, y, y1, y3, 0, head_ids, None)

    gathers[0].a()
    cot_gather.a()
    gathers[1].a()
    gathers[2].a()

    for h in range(HL):
        hs = pl.ds(h * DH, DH)
        qs[h, 0:FR, :] = fq[:, hs]
        qs[h, FR:R, :] = cq[pl.ds(pl.multiple_of(ctx * CR, CR), CR), hs]
    diag = lax.broadcasted_iota(jnp.int32, (128, 128), 0) == lax.broadcasted_iota(
        jnp.int32, (128, 128), 1
    )
    fsc_col = jnp.sum(jnp.where(diag, jnp.broadcast_to(fsc_row, (128, 128)), 0.0), axis=1, keepdims=True)
    csc_col = scale_of(lax.broadcasted_iota(jnp.int32, (CR, 1), 0) + ctx * CR, csz, 0)
    qsc = jnp.concatenate([fsc_col, csc_col], axis=0)
    ksc[:, 0:512] = scale_of(lax.broadcasted_iota(jnp.int32, (8, 512), 1), csz, 0)

    gathers[0].b()
    cot_gather.b()
    gathers[1].b()
    gathers[2].b()
    gathers[0].c()
    cot_gather.c()
    gathers[0].d()
    gathers[1].c()
    cot_gather.d()
    gathers[2].c()
    gathers[0].e()
    for slot in range(16):
        ksc[:, 512 + slot * 128 : 640 + slot * 128] = kv[0, slot, 256:272, :].astype(F32)[0:8]

    to_log2 = math.log2(math.e) / math.sqrt(DH)
    factor = 1.0 / math.sqrt(DH)

    def key_block(h, j):
        if j == 0:
            return ck[:, h * DH : (h + 1) * DH]
        return kv[h, 4 * (j - 1) : 4 * j, 0:128, :].reshape(512, DH)

    def value_block(h, j):
        if j == 0:
            return cv[:, h * DH : (h + 1) * DH]
        return kv[h, 4 * (j - 1) : 4 * j, 128:256, :].reshape(512, DH)

    inverse = [None] * HL

    def forward(h):
        q = qs[h]
        high = None
        for j in range(5):
            cols = slice(512 * j, 512 * (j + 1))
            s = dot(q, key_block(h, j), NT) * to_log2
            s = jnp.where(ksc[0:1, cols] <= qsc, s, NEG)
            tbuf[:, cols] = s
            top = jnp.max(s, axis=1, keepdims=True)
            high = top if high is None else jnp.maximum(high, top)
        total = jnp.zeros((R, 1), F32)
        acc = jnp.zeros((R, DH), F32)
        for j in range(5):
            cols = slice(512 * j, 512 * (j + 1))
            e = jnp.exp2(tbuf[:, cols] - high)
            total = total + jnp.sum(e, axis=1, keepdims=True)
            eb = e.astype(BF)
            ebuf[h, :, cols] = eb
            acc = acc + dot(eb, value_block(h, j), NN)
        inverse[h] = 1.0 / total
        attn_s[:, h * DH : (h + 1) * DH] = (acc * inverse[h]).astype(BF)

    def grad_attn():
        acc = jnp.zeros((R, HL * DH), F32)
        for slot in range(8):
            block = (slot % 2) * 4 + slot // 2
            acc = acc + dot(cotb[slot], w[:, block * 384 : (block + 1) * 384], NT)
        do_s[...] = acc.astype(BF)

    def weight_grad(h):
        a_t = attn_s[:, h * DH : (h + 1) * DH].astype(F32).T.astype(BF)
        for slot in range(8):
            g = dot(a_t, cotb[slot], NN).astype(BF)
            for half in range(2):
                for i in range(3):
                    part[h, half * 8 + slot, 320 + 64 * i : 384 + 64 * i, :] = g[
                        64 * half : 64 * half + 64, 128 * i : 128 * i + 128
                    ]

    def backward(h):
        cols_h = slice(h * DH, (h + 1) * DH)
        go = do_s[:, cols_h]
        gof = go.astype(F32)
        delta = jnp.sum(gof * attn_s[:, cols_h].astype(F32), axis=1, keepdims=True)
        c = inverse[h] * factor
        go_t = (gof * inverse[h]).T.astype(BF)
        q_t = qs[h].astype(F32).T.astype(BF)
        dq = jnp.zeros((R, DH), F32)
        for j in range(5):
            cols = slice(512 * j, 512 * (j + 1))
            dp = dot(go, value_block(h, j), NT)
            eb = ebuf[h, :, cols]
            ds = (eb.astype(F32) * ((dp - delta) * c)).astype(BF)
            dq = dq + dot(ds, key_block(h, j), NN)
            dk_t = dot(q_t, ds, NN)
            dv_t = dot(go_t, eb, NN)
            if j == 0:
                dk = dk_t.T.astype(BF)
                dv = dv_t.T.astype(BF)
                for slot in range(16):
                    at = ctx_of(slot) * CR
                    part[h, slot, 256:288, :] = dk[at : at + CR]
                    part[h, slot, 288:320, :] = dv[at : at + CR]
            else:
                for i in range(4):
                    slot = 4 * (j - 1) + i
                    part[h, slot, 0:128, :] = dk_t[:, 128 * i : 128 * i + 128].astype(BF)
                    part[h, slot, 128:256, :] = dv_t[:, 128 * i : 128 * i + 128].astype(BF)
        dqb = dq.astype(BF)
        fdq[:, cols_h] = dqb[0:FR]
        fbuf[pl.ds(own, 1), CR : 2 * CR, cols_h] = dqb[FR:R][None]

    class Scatter:
        def __init__(self, src, sibling, bufs, cut, pair, ring, ring1, ring2, ring3, first, ids):
            self.src, self.sibling, self.bufs, self.cut = src, sibling, bufs, cut
            self.pair, self.ring, self.ring1, self.ring2, self.ring3 = pair, ring, ring1, ring2, ring3
            self.first, self.ids = first, ids
            self.rows = src.shape[1]

        def add(self, slot, half, other):
            rows = pl.ds(0, self.cut) if half == 0 else pl.ds(self.cut, self.rows - self.cut)
            if half is None:
                rows = pl.ds(0, self.rows)
            v = self.src.at[pl.ds(slot, 2), rows]
            v[...] = (v[...].astype(F32) + other[...].astype(F32)).astype(BF)

        def a(self):
            if self.sibling is not None:
                peer, landing = self.sibling
                self.cs = send(self.src.at[pl.ds(8 - self.first, 8)], landing, peer)

        def b(self):
            if self.sibling is not None:
                self.cs.wait_recv()
                landing = self.sibling[1]
                for r in (self.ring2, self.ring1, self.ring3, self.ring):
                    self.add(self.first + r * 2, None, landing.at[pl.ds(r * 2, 2)])
                    if r is self.ring2:
                        self.send_far()
            else:
                self.send_far()

        def send_far(self):
            far = self.src.at[pl.ds(self.first + self.ring2 * 2, 2)]
            ta, tb = self.bufs[0], self.bufs[1]
            self.ca = send(far.at[:, pl.ds(0, self.cut)], ta, self.ids[1])
            self.cb = send(far.at[:, pl.ds(self.cut, self.rows - self.cut)], tb, self.ids[2])

        def c(self):
            self.ca.wait_recv()
            self.add(self.first + self.ring3 * 2, 0, self.bufs[0])
            self.c3 = send(self.src.at[pl.ds(self.first + self.ring3 * 2, 2)], self.bufs[3], self.ids[2])
            self.cb.wait_recv()
            self.add(self.first + self.ring1 * 2, 1, self.bufs[1])
            self.c1 = send(self.src.at[pl.ds(self.first + self.ring1 * 2, 2)], self.bufs[2], self.ids[1])

        def d(self):
            self.c1.wait_recv()
            self.c3.wait_recv()
            o = self.first + self.ring * 2
            other = 1 - self.pair

            def summed(p):
                return (
                    self.src[pl.ds(o + p, 1)].astype(F32)
                    + self.bufs[2][pl.ds(p, 1)].astype(F32)
                    + self.bufs[3][pl.ds(p, 1)].astype(F32)
                )

            self.src[pl.ds(o + other, 1)] = summed(other).astype(BF)
            self.cx = send(self.src.at[o + other], self.bufs[4], self.ids[0])
            self.mine = summed(self.pair)[0]

        def e(self):
            self.cx.wait_recv()
            return self.mine + self.bufs[4][...].astype(F32)

    scatters = [
        Scatter(
            part.at[h],
            (sib, sibr.at[h]),
            (ra.at[h], rb.at[h], r1.at[h], r3.at[h], rx.at[h]),
            256, xh, z, z1, z2, z3, core * 8, ctx_ids,
        )
        for h in range(HL)
    ]
    out_scatter = Scatter(
        opart, None, (ora, orb, or1, or3, orx), 80, xl, y, y1, y2, y3, 0, head_ids
    )

    forward(0)
    gathers[1].d()
    gathers[2].d()
    grad_attn()
    weight_grad(0)
    backward(0)
    scatters[0].a()
    gathers[1].e()
    forward(1)
    scatters[0].b()
    weight_grad(1)
    backward(1)
    scatters[0].c()
    scatters[1].a()
    gathers[2].e()
    forward(2)
    scatters[1].b()
    for slot in range(8):
        block = (slot % 2) * 4 + slot // 2
        opart[slot] = dot(attn_s[...], w[:, block * 384 : (block + 1) * 384], NN).astype(BF)
    out_scatter.b()
    weight_grad(2)
    scatters[0].d()
    backward(2)
    scatters[2].a()
    scatters[1].c()
    out_scatter.c()
    scatters[2].b()
    out_scatter.d()

    lane = lax.broadcasted_iota(jnp.int32, (64, 128), 1)

    def finish(h):
        total = scatters[h].e()
        cols_h = slice(h * DH, (h + 1) * DH)
        fdk[:, cols_h] = total[0:128].T.astype(BF)
        fdv[:, cols_h] = total[128:256].T.astype(BF)
        cdk[:, cols_h] = total[256:288].astype(BF)
        cdv[:, cols_h] = total[288:320].astype(BF)
        c0, c1, c2 = total[320:384], total[384:448], total[448:512]
        s1 = pltpu.roll(c1, 64, 1)
        s2 = pltpu.roll(c2, 64, 1)
        b0 = jnp.where(lane < 64, s1, s2)
        zero = core == 0
        keep0 = jnp.where(zero, c0, b0)
        keep1 = jnp.where(zero, c1, s2)
        wsend[h, :, 0:128] = jnp.where(zero, b0, c0)
        wsend[h, :, 128:256] = jnp.where(zero, s2, c1)
        rows = pl.ds(pl.multiple_of(h * DH + core * 64, 64), 64)
        wg[rows, 0:128] = keep0
        wg[rows, 128:192] = keep1[:, 0:64]
        return send(wsend.at[h], wrecv.at[h], sib)

    total = out_scatter
    w0 = finish(0)
    out_rows = total.e().astype(BF)
    fout[...] = out_rows[0:FR]
    fbuf[pl.ds(own, 1), 0:CR, :] = out_rows[FR:R][None]
    last = Gather(rows_at(fbuf, 32, 64), None, xh, z, z1, z3, core * 8, ctx_ids, sib)
    last.a()
    scatters[1].d()
    scatters[2].c()
    last.b()
    last.c()
    w1 = finish(1)
    scatters[2].d()
    last.d()
    w2 = finish(2)
    last.e()
    for slot in range(16):
        at = ctx_of(slot) * CR
        cout[at : at + CR, :] = fbuf[slot, 0:CR, :]
        cdq[at : at + CR, :] = fbuf[slot, CR : 2 * CR, :]
    for h, cw in enumerate((w0, w1, w2)):
        cw.wait_recv()
        rows = pl.ds(pl.multiple_of(h * DH + (1 - core) * 64, 64), 64)
        wg[rows, 0:128] = wrecv[h, :, 0:128]
        wg[rows, 128:192] = wrecv[h, :, 128:192]
    for copy in started:
        copy.wait_send()


def on_device(cq, ck, cv, fq, fk, fv, csz, fsz, fpos, w, cc, fc):
    vmem = pl.BlockSpec(memory_space=pltpu.VMEM)
    smem = pl.BlockSpec(memory_space=pltpu.SMEM)
    shapes = [
        ((512, 384), BF), ((128, 384), BF), ((512, 384), BF), ((32, 384), BF), ((32, 384), BF),
        ((128, 384), BF), ((128, 384), BF), ((128, 384), BF), ((384, 192), F32),
    ]
    v = pltpu.VMEM
    return pl.pallas_call(
        kernel,
        out_shape=[jax.ShapeDtypeStruct(s, d) for s, d in shapes],
        in_specs=[vmem] * 6 + [smem] * 2 + [vmem] * 4,
        out_specs=[vmem] * 9,
        scratch_shapes=[
            v((HL, R, DH), BF),
            v((HL, 16, KR, DH), BF),
            v((8, R, 384), BF),
            v((8, 2560), F32),
            v((R, 2560), F32),
            v((HL, R, 2560), BF),
            v((R, 384), BF),
            v((R, 384), BF),
            v((HL, 16, CH, DH), BF),
            v((HL, 8, CH, DH), BF),
            v((HL, 2, CH // 2, DH), BF),
            v((HL, 2, CH // 2, DH), BF),
            v((HL, 2, CH, DH), BF),
            v((HL, 2, CH, DH), BF),
            v((HL, CH, DH), BF),
            v((8, R, 384), BF),
            v((2, 80, 384), BF),
            v((2, 80, 384), BF),
            v((2, R, 384), BF),
            v((2, R, 384), BF),
            v((R, 384), BF),
            v((16, 2 * CR, 384), BF),
            v((HL, 64, 256), F32),
            v((HL, 64, 256), F32),
            pltpu.SemaphoreType.DMA((64,)),
            pltpu.SemaphoreType.DMA((64,)),
        ],
        compiler_params=pltpu.CompilerParams(
            collective_id=0, has_side_effects=True, vmem_limit_bytes=56 * 2**20
        ),
        cost_estimate=pl.CostEstimate(flops=7 * 10**9, bytes_accessed=8 * 10**6, transcendentals=1300000),
    )(cq, ck, cv, fq, fk, fv, csz, fsz, fpos.reshape(1, 128), w, cc, fc)


def solution(mesh):
    placed = (
        P(None, "head"), P(None, "head"), P(None, "head"),
        P("ctx", "head"), P("ctx", "head"), P("ctx", "head"),
        P(), P(), P("ctx"), P("head", None), P(None, "head"), P("ctx", "head"),
    )
    return jax.shard_map(
        on_device,
        mesh=mesh,
        in_specs=placed,
        out_specs=(
            P(None, "head"), P("ctx", "head"), P(None, "head"),
            P("ctx", "head"), P("ctx", "head"), P("ctx", "head"),
            P("ctx", "head"), P("ctx", "head"), P("head", "ctx"),
        ),
        check_vma=False,
    )
```

time: 670 us -> 93.3 us (0.14)
  waiting for transfers between devices: 279 us -> 0 us
  local copies, waits for them, and re-layouts: 211 us -> 10.2 us
  matrix products: 84.1 us -> 0 us
  Pallas kernels: 0 us -> 82.2 us
  blocking collectives: 54.4 us -> 0 us
  other arithmetic: 19.2 us -> 0 us
  between operations: 14.6 us -> 0.7 us
    reduce_scatter x7 -> x0, waiting for transfers between devices: 261 us -> none  [the longest x1 83.1 us: on_device(): lax.psum_scatter(weight_grad, 'ctx', scatter_dimension=1, tiled=True)]
    dynamic_update_slice x16 -> x0, local copies, waits for them, and re-layouts: 150 us -> none  [backward(): lax.scan(backward_advance, jnp.zeros(query3.shape, jnp.float32), key_group)]
    dot_general x45 -> x0, matrix products: 84.1 us -> none  [the longest x6 12.8 us: attend_advance(): jnp.einsum('hqk,khd->qhd', weights, value_block, preferred_element_type=j...]
    pallas_call x0 -> x1, Pallas kernels: none -> 82.2 us  [on_device(): pl.pallas_call(kernel, out_shape=[jax.ShapeDtypeStruct(s, d) for s, d in...]
    all_gather x2 -> x0, blocking collectives: 54.4 us -> none  [the longest x1 27.8 us: on_device(): fine_piece = lax.all_gather(fine_cotangent, 'head', axis=1, tiled=True)]
    unnamed x58 -> x18, local copies, waits for them, and re-layouts: 29.4 us -> 8.26 us
    all_gather x3 -> x0, waiting for transfers between devices: 16.1 us -> none  [the longest x1 16.1 us: on_device(): lax.all_gather(fine_value, 'ctx', axis=0, tiled=True)]
    reshape x4 -> x0, local copies, waits for them, and re-layouts: 12.5 us -> none  [the longest x1 5.13 us: blocked(): key_rows.reshape(block_count, block_width, head_count, DH)]
  transfers between devices with their start and end apart: 10 -> 0, of which waited for: 5 -> 0; matrix products, arithmetic and copies ran while one was open for 47% -> 0% of each run, Pallas kernels for 0% -> 0%
where the time goes in v1:
time: 93.3 us; the launch traced here: 93.1 us
  Pallas kernels  82.2 us (88%)
  local copies, waits for them, and re-layouts  10.2 us (11%)
    pallas_call x1, Pallas kernels, on_device(): pl.pallas_call(kernel, out_shape=[jax.ShapeDtypeStruct(s, d) for s, d in...  82.2 us
    unnamed x18, local copies, waits for them, and re-layouts  8.26 us
    pallas_call x1, local copies, waits for them, and re-layouts, on_device(): pl.pallas_call(kernel, out_shape=[jax.ShapeDtypeStruct(s, d) for s, d in...  1.91 us

profile of v1, /device:TPU:1, one launch (start us, length us, event | category | flops | bytes accessed | tf_op | source)
XLA Modules:
  0.0 93.1 jit_solution(9365226070604239820)
XLA Ops:
  0.6 82.2 %shard_map.187 = (bf16[512,384]{1,0:T(8,128)(2,1)}, bf16[128,384]{1,0:T(8,128)(2,1)}, bf16[512,384]{1,0:T(8,128)(2,1)}, bf16[32,384]{1,0:T(8,128)(2,1)}, bf16[32...) custom-call(bf16[512,384]{1,0:T(8,128)(2,1)} %cq.1, ...), custom_call_target="tpu_custom_call" | custom-call | flops 7000000000 | bytes 8000000 | tf_op jit(solution)/shard_map/pallas_call | solution.py:451
  82.9 0.0 copy-start.4
  82.9 0.0 copy-start.3
  82.9 0.0 copy-start.2
  82.9 0.0 copy-start.1
  82.9 0.0 copy-start
  82.9 1.9 %copy.21 = f32[384,192]{0,1:T(8,128)} copy(f32[384,192]{1,0:T(8,128)} %get-tuple-element.17) | data formatting | bytes 589824 | tf_op jit(solution)/shard_map/pallas_call | solution.py:451
  84.8 1.8 %copy.30 = bf16[512,384]{1,0:T(8,128)(2,1)} copy(bf16[512,384]{1,0:T(8,128)(2,1)} %get-tuple-element.27) | data formatting | bytes 786432
  86.6 1.5 %copy.31 = bf16[128,384]{1,0:T(8,128)(2,1)} copy(bf16[128,384]{1,0:T(8,128)(2,1)} %get-tuple-element.28) | data formatting | bytes 196608
  88.2 1.8 %copy.32 = bf16[512,384]{1,0:T(8,128)(2,1)} copy(bf16[512,384]{1,0:T(8,128)(2,1)} %get-tuple-element.29) | data formatting | bytes 786432
  89.9 0.0 copy-done.4
  89.9 0.6 copy.33
  90.5 0.0 copy-done.3
  90.5 0.6 copy.34
  91.2 0.0 copy-done.2
  91.2 0.6 copy.35
  91.8 0.0 copy-done.1
  91.8 0.6 copy.36
  92.4 0.0 copy-done
  92.4 0.6 copy.37
Async XLA Ops:
  82.9 7.1 %copy-start.4 = (bf16[32,384]{1,0:T(8,128)(2,1)S(1)}, bf16[32,384]{1,0:T(8,128)(2,1)}, u32[]{:S(2)}) copy-start(bf16[32,384]{1,0:T(8,128)(2,1)} %get-tuple-element.30) | copy-start | bytes 73732
  82.9 7.7 %copy-start.3 = (bf16[32,384]{1,0:T(8,128)(2,1)S(1)}, bf16[32,384]{1,0:T(8,128)(2,1)}, u32[]{:S(2)}) copy-start(bf16[32,384]{1,0:T(8,128)(2,1)} %get-tuple-element.31) | copy-start | bytes 73732
  82.9 8.3 %copy-start.2 = (bf16[128,384]{1,0:T(8,128)(2,1)S(1)}, bf16[128,384]{1,0:T(8,128)(2,1)}, u32[]{:S(2)}) copy-start(bf16[128,384]{1,0:T(8,128)(2,1)} %get-tuple-element.32) | copy-start | bytes 294916
  82.9 8.9 %copy-start.1 = (bf16[128,384]{1,0:T(8,128)(2,1)S(1)}, bf16[128,384]{1,0:T(8,128)(2,1)}, u32[]{:S(2)}) copy-start(bf16[128,384]{1,0:T(8,128)(2,1)} %get-tuple-element.33) | copy-start | bytes 294916
  82.9 9.5 %copy-start = (bf16[128,384]{1,0:T(8,128)(2,1)S(1)}, bf16[128,384]{1,0:T(8,128)(2,1)}, u32[]{:S(2)}) copy-start(bf16[128,384]{1,0:T(8,128)(2,1)} %get-tuple-element.34) | copy-start | bytes 294916

commit v2 on v1

v2 whole, which is shorter than its diff:
```python
import math

import jax
import jax.numpy as jnp
from jax import lax
from jax.experimental import pallas as pl
from jax.experimental.pallas import tpu as pltpu
from jax.sharding import PartitionSpec as P

DH = 128
HL = 3
FR = 128
CR = 32
R = FR + CR
KR = 272
CA = 320
CW = 192
HALF = 256
NEG = -1e30
BF = jnp.bfloat16
F32 = jnp.float32
MESH = pl.DeviceIdType.MESH
NT = (((1,), (1,)), ((), ()))
TN = (((0,), (0,)), ((), ()))
NN = (((1,), (0,)), ((), ()))


def dot(a, b, dims):
    return lax.dot_general(a, b, dims, preferred_element_type=F32)


def kernel(
    cq, ck_in, cv_in, fq, fk, fv, csz, fsz, fpos, w_in, cc, fc,
    fout_o, fdq_o, fdk_o, fdv_o, cdk_o, cdv_o, wg_o, obuf_o, qbuf_o,
    ck, cv, w, q2, qc, kv, cotb, scx, ksc, tbuf, ebuf, ecds, ecx, attn_all, do_c, gcn, gcx, do2,
    on_s, on_r, st_s, st_r, dq_s, dq_r,
    pa, pw, sa, sw, az, wz, wx,
    oc, ocr, ocx, of, ofr, ofx, obuf, qbuf, wsend, wrecv,
    fout, fdq, fdk, fdv, cdk, cdv, wg,
    ssem, rsem, isem, osem,
):
    ctx = lax.axis_index("ctx")
    head = lax.axis_index("head")
    core = ctx % 2
    z = (ctx // 2) % 4
    xh = ctx // 8
    y = head % 4
    xl = head // 4
    z1 = z + 1 - 2 * (z % 2)
    z3 = 3 - z
    z2 = (z + 2) % 4
    y1 = y + 1 - 2 * (y % 2)
    y3 = 3 - y
    y2 = (y + 2) % 4

    def ctx_id(a, b, c):
        return ((a * 4 + b) * 2 + c, head)

    sib = ctx_id(xh, z, 1 - core)
    px = ctx_id(1 - xh, z, core)
    pz1 = ctx_id(xh, z1, core)
    pz3 = ctx_id(xh, z3, core)
    py1 = (ctx, xl * 4 + y1)
    py3 = (ctx, xl * 4 + y3)
    py2 = (ctx, xl * 4 + y2)
    pz2 = ctx_id(xh, z2, core)
    pxl = (ctx, (1 - xl) * 4 + y)
    peers = (px, pz2, pz3, pz1, py2, py3, py1, pxl, sib)

    barrier = pltpu.get_barrier_semaphore()
    for peer in peers:
        pl.semaphore_signal(barrier, inc=1, device_id=peer, device_id_type=MESH)

    loads = [0]

    def load(src, dst):
        copy = pltpu.make_async_copy(src, dst, isem.at[loads[0]])
        loads[0] += 1
        copy.start()
        return copy

    share = pl.ds(pl.multiple_of(ctx * CR, CR), CR)
    pair_share = pl.ds(pl.multiple_of((((1 - xh) * 4 + z) * 2 + core) * CR, CR), CR)
    in_kv = []
    for h in range(HL):
        hs = pl.ds(h * DH, DH)
        in_kv.append((load(fk.at[:, hs], kv.at[h, core, z, pl.ds(0, 128)]), load(fv.at[:, hs], kv.at[h, core, z, pl.ds(128, 128)])))
        if h == 0:
            in_cot = (load(fc, cotb.at[y, xl, pl.ds(0, FR)]), load(cc.at[share], cotb.at[y, xl, pl.ds(FR, CR)]))
    in_q = []
    for h in range(HL):
        hs = pl.ds(h * DH, DH)
        in_q.append((load(fq.at[:, hs], q2.at[h, pl.ds(0, FR)]), load(cq.at[share, hs], qc.at[h, pl.ds(0, CR)]), load(cq.at[pair_share, hs], qc.at[h, pl.ds(CR, CR)])))
    in_ck = load(ck_in, ck)
    in_cv = load(cv_in, cv)
    in_w = load(w_in, w)

    def scale_of(position, sizes, first):
        end = jnp.int32(0)
        total = jnp.zeros(position.shape, jnp.int32) + first
        for s in range(6):
            end = end + sizes[s]
            total = total + (position >= end).astype(jnp.int32)
        return total.astype(F32)

    fsc_row = scale_of(fpos[...], fsz, 6)
    for h in range(HL):
        kv[h, core, z, 256:272, :] = jnp.broadcast_to(fsc_row, (16, 128)).astype(BF)

    count = [0]
    started = []

    def send(src, dst, peer):
        i = count[0]
        count[0] += 1
        copy = pltpu.make_async_remote_copy(
            src_ref=src,
            dst_ref=dst,
            send_sem=ssem.at[i],
            recv_sem=rsem.at[i],
            device_id=peer,
            device_id_type=MESH,
        )
        copy.start()
        started.append(copy)
        return copy

    rings = (z2, z1, z3)
    pz = (pz2, pz1, pz3)
    py = (py2, py1, py3)

    class Gather:
        def __init__(self, at, all_of, ring, pair, ids, pair_id, sibling):
            self.at, self.all_of, self.ring, self.pair = at, all_of, ring, pair
            self.ids, self.pair_id, self.sibling = ids, pair_id, sibling

        def a(self):
            v = self.at(self.ring, self.pair)
            if self.pair_id is not None:
                self.cx = send(v, v, self.pair_id)
            self.waits = [send(v, v, peer) for peer in self.ids]

        def b(self):
            self.cx.wait_recv()
            v = self.at(self.ring, 1 - self.pair)
            self.waits += [send(v, v, peer) for peer in self.ids]

        def d(self):
            for copy in self.waits:
                copy.wait_recv()
            if self.sibling is not None:
                self.cs = send(self.all_of, self.all_of, self.sibling)

        def e(self):
            self.cs.wait_recv()

    gathers = [
        Gather((lambda h: lambda r, p: kv.at[h, core, r])(h), kv.at[h, core], z, None, pz, None, sib)
        for h in range(HL)
    ]
    cot_gather = Gather(lambda r, p: cotb.at[r, p], None, y, xl, py, pxl, None)
    out_gather = Gather(lambda r, p: obuf.at[core, r, p], obuf.at[core], z, xh, pz, px, sib)
    dq_gather = Gather(lambda r, p: qbuf.at[core, r, p], qbuf.at[core], z, xh, pz, px, sib)

    pl.semaphore_wait(barrier, len(peers))

    def gather_a(h):
        for copy in in_kv[h]:
            copy.wait()
        gathers[h].a()

    for copy in in_cot:
        copy.wait()
    cot_gather.a()
    gather_a(0)
    for copy in in_q[0] + in_q[1] + in_q[2]:
        copy.wait()
    own_rows, pair_rows = pl.ds(0, FR), pl.ds(FR, FR)
    c_scale = send(kv.at[0, core, z, pl.ds(256, 16)], scx, px)
    c_query = send(q2.at[:, own_rows], q2.at[:, pair_rows], px)

    diag = lax.broadcasted_iota(jnp.int32, (128, 128), 0) == lax.broadcasted_iota(
        jnp.int32, (128, 128), 1
    )

    def column(row):
        return jnp.sum(jnp.where(diag, jnp.broadcast_to(row, (128, 128)), 0.0), axis=1, keepdims=True)

    fsc_col = column(fsc_row)
    csc_col = scale_of(lax.broadcasted_iota(jnp.int32, (CR, 1), 0) + ctx * CR, csz, 0)
    csc_row = scale_of(lax.broadcasted_iota(jnp.int32, (1, 512), 1), csz, 0)

    to_log2 = math.log2(math.e) / math.sqrt(DH)
    factor = 1.0 / math.sqrt(DH)
    planes = (1 - core, core)

    blocks = (slice(0, 256), slice(256, 768), slice(768, 1280))
    half_rows = pl.ds(pl.multiple_of(xh * HALF, HALF), HALF)

    def key_block(h, j):
        if j == 0:
            return ck[half_rows, h * DH : (h + 1) * DH]
        return kv[h, planes[j - 1], :, 0:128, :].reshape(512, DH)

    def value_block(h, j):
        if j == 0:
            return cv[half_rows, h * DH : (h + 1) * DH]
        return kv[h, planes[j - 1], :, 128:256, :].reshape(512, DH)

    inverse = [None] * HL
    inverse_c = [None] * HL
    high = [None] * HL
    total = [None] * HL
    row_scale = [None]

    def coarse_forward(h):
        cols_h = slice(h * DH, (h + 1) * DH)
        s = dot(qc[h, 0:CR, :], ck[:, cols_h], NT) * to_log2
        s = jnp.where(csc_row <= csc_col, s, NEG)
        e = jnp.exp2(s - jnp.max(s, axis=1, keepdims=True))
        inverse_c[h] = 1.0 / jnp.sum(e, axis=1, keepdims=True)
        eb = e.astype(BF)
        for i in range(2):
            ecds[h, i, 0] = eb[:, HALF * i : HALF * (i + 1)]
        acc = dot(eb, cv[:, cols_h], NN)
        attn_all[FR:R, cols_h] = (acc * inverse_c[h]).astype(BF)

    def forward(h):
        m = None
        for j, cols in enumerate(blocks):
            s = dot(q2[h], key_block(h, j), NT) * to_log2
            if j > 0:
                s = jnp.where(ksc[0:1, cols.start - 256 : cols.stop - 256] <= row_scale[0], s, NEG)
            tbuf[h, :, cols] = s
            top = jnp.max(s, axis=1, keepdims=True)
            m = top if m is None else jnp.maximum(m, top)
        l = jnp.zeros((2 * FR, 1), F32)
        acc = jnp.zeros((2 * FR, DH), F32)
        for j, cols in enumerate(blocks):
            e = jnp.exp2(tbuf[h, :, cols] - m)
            l = l + jnp.sum(e, axis=1, keepdims=True)
            eb = e.astype(BF)
            ebuf[h, :, cols] = eb
            acc = acc + dot(eb, value_block(h, j), NN)
        high[h], total[h] = m, l
        on_s[h] = (acc * (1.0 / l)).astype(BF)
        lane2 = lax.broadcasted_iota(jnp.int32, (2 * FR, 128), 1)
        st_s[h] = jnp.where(lane2 == 0, m, l).T[0:8]
        return send(on_s.at[h], on_r.at[h], px), send(st_s.at[h], st_r.at[h], px)

    def swapped(v):
        return jnp.concatenate([v[FR:], v[:FR]], axis=0)

    def combine(h, copies):
        for copy in copies:
            copy.wait_recv()
        st = swapped(jnp.concatenate([st_r[h]] * 16, axis=0).T)
        m2, l2 = st[:, 0:1], st[:, 1:2]
        m1, l1 = high[h], total[h]
        m = jnp.maximum(m1, m2)
        f1 = jnp.exp2(m1 - m)
        w1, w2 = l1 * f1, l2 * jnp.exp2(m2 - m)
        rl = 1.0 / (w1 + w2)
        inverse[h] = f1 * rl
        both = on_s[h].astype(F32) * (w1 * rl) + swapped(on_r[h].astype(F32)) * (w2 * rl)
        both = both.astype(BF)
        cols_h = slice(h * DH, (h + 1) * DH)
        attn_all[0:FR, cols_h] = both[0:FR]
        attn_all[R : R + FR, cols_h] = both[FR:]

    def grad_attn():
        acc = jnp.zeros((R, HL * DH), F32)
        for block in range(8):
            acc = acc + dot(cotb[block % 4, block // 4], w[:, block * 384 : (block + 1) * 384], NT)
        acc = acc.astype(BF)
        do2[0:FR, :] = acc[0:FR]
        do_c[...] = acc[FR:R]
        return send(do2.at[own_rows], do2.at[pair_rows], px)

    def weight_grad(h):
        a_t = attn_all[0:R, h * DH : (h + 1) * DH].astype(F32).T.astype(BF)
        for block in range(8):
            p, r = divmod(block, 4)
            g = dot(a_t, cotb[r, p], NN).astype(BF)
            for half in range(2):
                for i in range(3):
                    pw[h, half, r, p, 64 * i : 64 * i + 64, :] = g[
                        64 * half : 64 * half + 64, 128 * i : 128 * i + 128
                    ]

    def coarse_project():
        for block in range(8):
            oc[block % 4, block // 4] = dot(
                attn_all[FR:R, :], w[:, block * 384 : (block + 1) * 384], NN
            ).astype(BF)

    def fine_project():
        for block in range(8):
            of[block % 4, block // 4] = dot(
                attn_all[0:FR, :], w[:, block * 384 : (block + 1) * 384], NN
            ).astype(BF)

    def coarse_backward(h):
        cols_h = slice(h * DH, (h + 1) * DH)
        go = do_c[:, cols_h]
        gof = go.astype(F32)
        delta = jnp.sum(gof * attn_all[FR:R, cols_h].astype(F32), axis=1, keepdims=True)
        gcn[:, cols_h] = (gof * inverse_c[h]).astype(BF)
        dp = dot(go, cv[:, cols_h], NT)
        eb = jnp.concatenate([ecds[h, 0, 0], ecds[h, 1, 0]], axis=1)
        ds = (eb.astype(F32) * ((dp - delta) * (inverse_c[h] * factor))).astype(BF)
        for i in range(2):
            ecds[h, i, 1] = ds[:, HALF * i : HALF * (i + 1)]
        qbuf[core, z, xh, :, cols_h] = dot(ds, ck[:, cols_h], NN).astype(BF)

    def backward(h):
        cols_h = slice(h * DH, (h + 1) * DH)
        go = do2[:, cols_h]
        gof = go.astype(F32)
        attn = jnp.concatenate([attn_all[0:FR, cols_h], attn_all[R : R + FR, cols_h]], axis=0)
        delta = jnp.sum(gof * attn.astype(F32), axis=1, keepdims=True)
        c = inverse[h] * factor
        go_n = (gof * inverse[h]).T.astype(BF)
        q_t = q2[h].astype(F32).T.astype(BF)
        dq = jnp.zeros((2 * FR, DH), F32)
        for j, cols in enumerate(blocks):
            dp = dot(go, value_block(h, j), NT)
            eb = ebuf[h, :, cols]
            ds = (eb.astype(F32) * ((dp - delta) * c)).astype(BF)
            dq = dq + dot(ds, key_block(h, j), NN)
            dk_t = dot(q_t, ds, NN)
            dv_t = dot(go_n, eb, NN)
            if j == 0:
                c_e = jnp.concatenate([ecds[h, xh, 0], ecx[h, 0]], axis=0)
                c_ds = jnp.concatenate([ecds[h, xh, 1], ecx[h, 1]], axis=0)
                c_go = jnp.concatenate([gcn[:, cols_h], gcx[:, cols_h]], axis=0)
                dk = (dk_t.T + dot(c_ds, qc[h], TN)).astype(BF)
                dv = (dv_t.T + dot(c_e, c_go, TN)).astype(BF)
                for r in range(4):
                    for cx in range(2):
                        at = (r * 2 + cx) * CR
                        pa[h, cx, r, 256:288, :] = dk[at : at + CR]
                        pa[h, cx, r, 288:320, :] = dv[at : at + CR]
            else:
                dk_t, dv_t = dk_t.astype(BF), dv_t.astype(BF)
                for r in range(4):
                    pa[h, planes[j - 1], r, 0:128, :] = dk_t[:, 128 * r : 128 * r + 128]
                    pa[h, planes[j - 1], r, 128:256, :] = dv_t[:, 128 * r : 128 * r + 128]
            yield
        fdq_own[h] = dq[0:FR]
        dq_s[:, cols_h] = dq[FR:].astype(BF)

    fdq_own = [None] * HL

    def up(value):
        return value.astype(F32)

    class RingFirst:
        def __init__(self, mine, from_ring, from_pair, rings, ring, pair, ids, pair_id):
            self.mine, self.from_ring, self.from_pair = mine, from_ring, from_pair
            self.rings, self.ring, self.pair, self.ids, self.pair_id = rings, ring, pair, ids, pair_id

        def b(self):
            self.cr = [
                send(self.mine.at[r], self.from_ring.at[i], self.ids[i]) for i, r in enumerate(self.rings)
            ]

        def c(self):
            for copy in self.cr:
                copy.wait_recv()

            def total(p):
                value = up(self.mine[self.ring, p])
                for i in range(3):
                    value = value + up(self.from_ring[i, p])
                return value

            self.mine[self.ring, 1 - self.pair] = total(1 - self.pair).astype(BF)
            self.cx = send(self.mine.at[self.ring, 1 - self.pair], self.from_pair, self.pair_id)
            self.kept = total(self.pair)

        def d(self):
            self.cx.wait_recv()
            return self.kept + up(self.from_pair[...])

    class RingOnly:
        def __init__(self, src, from_sib, from_ring):
            self.src, self.from_sib, self.from_ring = src, from_sib, from_ring

        def a(self):
            self.cs = send(self.src[0], self.from_sib, sib)

        def b(self):
            mine = self.src[1]
            self.cs.wait_recv()
            self.cr = []
            for i, r in enumerate(rings):
                mine[r] = (up(mine[r]) + up(self.from_sib[r])).astype(BF)
                self.cr.append(send(mine.at[r], self.from_ring.at[i], pz[i]))
            self.kept = up(mine[z]) + up(self.from_sib[z])

        def d(self):
            value = self.kept
            for i in range(3):
                self.cr[i].wait_recv()
                value = value + up(self.from_ring[i])
            return value

    class PairFirst:
        def __init__(self, src, from_sib, from_ring, from_pair):
            self.src, self.from_sib, self.from_ring, self.from_pair = src, from_sib, from_ring, from_pair

        def a(self):
            self.cs = send(self.src[0], self.from_sib, sib)

        def b(self):
            mine = self.src[1]
            self.cs.wait_recv()
            p = 1 - xh
            for r in range(4):
                mine[r, p] = (up(mine[r, p]) + up(self.from_sib[r, p])).astype(BF)
            self.cx = send(mine.at[:, p], self.from_pair, px)

        def c(self):
            mine = self.src[1]
            self.cx.wait_recv()

            def total(r):
                return up(mine[r, xh]) + up(self.from_sib[r, xh]) + up(self.from_pair[r])

            self.cr = []
            for i, r in enumerate(rings):
                mine[r, xh] = total(r).astype(BF)
                self.cr.append(send(mine.at[r, xh], self.from_ring.at[i], pz[i]))
            self.kept = total(z)

        def d(self):
            value = self.kept
            for i in range(3):
                self.cr[i].wait_recv()
                value = value + up(self.from_ring[i])
            return value

    sums_a = [RingOnly((pa.at[h, 1 - core], pa.at[h, core]), sa.at[h], az.at[h]) for h in range(HL)]
    sums_w = [
        PairFirst((pw.at[h, 1 - core], pw.at[h, core]), sw.at[h], wz.at[h], wx.at[h]) for h in range(HL)
    ]
    coarse_sum = RingFirst(oc, ocr, ocx, (y2, y1, y3), y, xl, py, pxl)
    fine_sum = RingFirst(of, ofr, ofx, (y2, y1, y3), y, xl, py, pxl)

    out_copies = []

    def store(src, dst):
        copy = pltpu.make_async_copy(src, dst, osem.at[len(out_copies)])
        out_copies.append(copy)
        copy.start()

    lane = lax.broadcasted_iota(jnp.int32, (192, 128), 1)

    def finish_a(h):
        total = sums_a[h].d()
        cols_h = slice(h * DH, (h + 1) * DH)
        fdk[:, cols_h] = total[0:128].T.astype(BF)
        fdv[:, cols_h] = total[128:256].T.astype(BF)
        cdk[:, cols_h] = total[256:288].astype(BF)
        cdv[:, cols_h] = total[288:320].astype(BF)

    def finish_w():
        for h in range(HL):
            total = sums_w[h].d()
            for i in range(3):
                piece = total[64 * i : 64 * i + 64]
                wsend[h, 128 * i : 128 * i + 128, :] = jnp.concatenate([piece, piece], axis=0).T
        other = pl.ds(pl.multiple_of((1 - core) * 192, 64), 192)
        return send(wsend.at[:, other], wrecv, sib)

    def finish_weight(copy):
        copy.wait_recv()
        for h in range(HL):
            mine = wsend[h, pl.ds(pl.multiple_of(core * 192, 64), 192), :]
            wg[:, h * DH : (h + 1) * DH] = jnp.where((lane < 64) == (core == 0), mine, wrecv[h])

    def coarse_done():
        obuf[core, z, xh] = coarse_sum.d().astype(BF)
        out_gather.a()

    def fine_done():
        fout[...] = fine_sum.d().astype(BF)
        store(fout, fout_o)

    def run(steps, events=()):
        todo = list(events)
        for i, _ in enumerate(steps):
            while todo and todo[0][0] <= i:
                todo.pop(0)[1]()
        for _, event in todo:
            event()

    g, A, W = gathers, sums_a, sums_w
    in_ck.wait()
    in_cv.wait()
    for h in range(HL):
        coarse_forward(h)
    gather_a(1)
    in_w.wait()
    coarse_project()
    coarse_sum.b()
    cot_gather.b()
    gather_a(2)
    g[0].d()
    c_scale.wait_recv()
    row_scale[0] = jnp.concatenate([fsc_col, column(scx[...].astype(F32)[0:1])], axis=0)
    c_query.wait_recv()
    g[0].e()
    for i in range(2):
        for r in range(4):
            at = (4 * i + r) * 128
            ksc[:, at : at + 128] = kv[0, planes[i], r, 256:272, :].astype(F32)[0:8]
    x0 = forward(0)
    g[1].d()
    coarse_sum.c()
    g[1].e()
    x1 = forward(1)
    g[2].d()
    cot_gather.d()
    c_do = grad_attn()
    g[2].e()
    x2 = forward(2)
    for h in range(HL):
        coarse_backward(h)
    c_ec = send(ecds.at[:, 1 - xh], ecx, px)
    c_gc = send(gcn, gcx, px)
    combine(0, x0)
    weight_grad(0)
    W[0].a()
    coarse_done()
    dq_gather.a()
    combine(1, x1)
    weight_grad(1)
    W[1].a()
    c_do.wait_recv()
    c_ec.wait_recv()
    c_gc.wait_recv()
    run(backward(0), [(1, A[0].a)])
    W[0].b()
    combine(2, x2)
    weight_grad(2)
    W[2].a()
    A[0].b()
    run(backward(1), [(1, A[1].a)])
    W[1].b()
    fine_project()
    fine_sum.b()
    A[1].b()
    run(backward(2), [(1, A[2].a)])
    W[2].b()
    c_dq = send(dq_s, dq_r, px)
    A[2].b()
    W[0].c()
    out_gather.b()
    dq_gather.b()
    finish_a(0)
    W[1].c()
    out_gather.d()
    dq_gather.d()
    finish_a(1)
    W[2].c()
    fine_sum.c()
    finish_a(2)
    store(fdk, fdk_o)
    store(fdv, fdv_o)
    store(cdk, cdk_o)
    store(cdv, cdv_o)
    c_dq.wait_recv()
    for h in range(HL):
        cols_h = slice(h * DH, (h + 1) * DH)
        fdq[:, cols_h] = (fdq_own[h] + up(dq_r[:, cols_h])).astype(BF)
    store(fdq, fdq_o)
    out_gather.e()
    store(obuf, obuf_o)
    dq_gather.e()
    store(qbuf, qbuf_o)
    c_w = finish_w()
    fine_done()
    finish_weight(c_w)
    store(wg, wg_o)
    for copy in started:
        copy.wait_send()
    for copy in out_copies:
        copy.wait()


def place(fout, fdq, fdk, fdv, cdk, cdv, wg, obuf, qbuf, *rest):
    outs, held, sem_in, sem_out = rest[:9], rest[9:18], rest[18], rest[19]
    loads = [[] for _ in outs]
    for i, src in ((1, fout), (3, cdk), (4, cdv), (5, fdq), (6, fdk), (7, fdv), (8, wg)):
        loads[i].append((src, held[i]))
    for core in range(2):
        for xh in range(2):
            loads[0].append((obuf.at[core, :, xh], held[0].at[xh, :, core]))
            loads[2].append((qbuf.at[core, :, xh], held[2].at[xh, :, core]))
    order = (0, 2, 8, 1, 5, 6, 7, 3, 4)
    copies = {}
    count = 0
    for i in order:
        copies[i] = []
        for src, dst in loads[i]:
            copies[i].append(pltpu.make_async_copy(src, dst, sem_in.at[count]))
            copies[i][-1].start()
            count += 1
    stores = []
    for i in order:
        for copy in copies[i]:
            copy.wait()
        stores.append(pltpu.make_async_copy(held[i], outs[i], sem_out.at[i]))
        stores[-1].start()
    for copy in stores:
        copy.wait()


def on_device(cq, ck, cv, fq, fk, fv, csz, fsz, fpos, w, cc, fc):
    vmem = pl.BlockSpec(memory_space=pltpu.VMEM)
    smem = pl.BlockSpec(memory_space=pltpu.SMEM)
    hbm = pl.BlockSpec(memory_space=pl.ANY)
    shapes = [
        ((128, 384), BF), ((128, 384), BF), ((128, 384), BF), ((128, 384), BF), ((32, 384), BF),
        ((32, 384), BF), ((192, 384), F32), ((2, 4, 2, CR, 384), BF), ((2, 4, 2, CR, 384), BF),
    ]
    v = pltpu.VMEM
    raw = pl.pallas_call(
        kernel,
        out_shape=[jax.ShapeDtypeStruct(s, d) for s, d in shapes],
        in_specs=[hbm] * 6 + [smem] * 2 + [vmem] + [hbm] * 3,
        out_specs=[hbm] * 9,
        scratch_shapes=[
            v((512, 384), BF),
            v((512, 384), BF),
            v((384, 3072), BF),
            v((HL, 2 * FR, DH), BF),
            v((HL, 2 * CR, DH), BF),
            v((HL, 2, 4, KR, DH), BF),
            v((4, 2, R, 384), BF),
            v((16, DH), BF),
            v((8, 1024), F32),
            v((HL, 2 * FR, 1280), F32),
            v((HL, 2 * FR, 1280), BF),
            v((HL, 2, 2, CR, HALF), BF),
            v((HL, 2, CR, HALF), BF),
            v((2 * R, 384), BF),
            v((CR, 384), BF),
            v((CR, 384), BF),
            v((CR, 384), BF),
            v((2 * FR, 384), BF),
            v((HL, 2 * FR, DH), BF),
            v((HL, 2 * FR, DH), BF),
            v((HL, 8, 2 * FR), F32),
            v((HL, 8, 2 * FR), F32),
            v((FR, 384), BF),
            v((FR, 384), BF),
            v((HL, 2, 4, CA, DH), BF),
            v((HL, 2, 4, 2, CW, DH), BF),
            v((HL, 4, CA, DH), BF),
            v((HL, 4, 2, CW, DH), BF),
            v((HL, 3, CA, DH), BF),
            v((HL, 3, CW, DH), BF),
            v((HL, 4, CW, DH), BF),
            v((4, 2, CR, 384), BF),
            v((3, 2, CR, 384), BF),
            v((CR, 384), BF),
            v((4, 2, FR, 384), BF),
            v((3, 2, FR, 384), BF),
            v((FR, 384), BF),
            v((2, 4, 2, CR, 384), BF),
            v((2, 4, 2, CR, 384), BF),
            v((HL, 384, 128), F32),
            v((HL, 192, 128), F32),
            v((128, 384), BF),
            v((128, 384), BF),
            v((128, 384), BF),
            v((128, 384), BF),
            v((32, 384), BF),
            v((32, 384), BF),
            v((192, 384), F32),
            pltpu.SemaphoreType.DMA((96,)),
            pltpu.SemaphoreType.DMA((96,)),
            pltpu.SemaphoreType.DMA((24,)),
            pltpu.SemaphoreType.DMA((9,)),
        ],
        compiler_params=pltpu.CompilerParams(
            collective_id=0, has_side_effects=True, vmem_limit_bytes=56 * 2**20
        ),
        cost_estimate=pl.CostEstimate(flops=7 * 10**9, bytes_accessed=8 * 10**6, transcendentals=1300000),
    )(cq, ck, cv, fq, fk, fv, csz, fsz, fpos.reshape(1, 128), w, cc, fc)
    coarse = ((2, 4, 2, CR, 384), BF)
    fine = ((128, 384), BF)
    small = ((32, 384), BF)
    placed = [coarse, fine, coarse, small, small, fine, fine, fine, ((192, 384), F32)]
    outs = pl.pallas_call(
        place,
        out_shape=[jax.ShapeDtypeStruct(s, d) for s, d in placed],
        in_specs=[hbm] * 9,
        out_specs=[hbm] * 9,
        scratch_shapes=[pltpu.VMEM(s, d) for s, d in placed]
        + [pltpu.SemaphoreType.DMA((15,)), pltpu.SemaphoreType.DMA((9,))],
    )(*raw)
    outs = list(outs)
    outs[0] = outs[0].reshape(512, 384)
    outs[2] = outs[2].reshape(512, 384)
    outs[8] = outs[8].T
    return tuple(outs)


def solution(mesh):
    placed = (
        P(None, "head"), P(None, "head"), P(None, "head"),
        P("ctx", "head"), P("ctx", "head"), P("ctx", "head"),
        P(), P(), P("ctx"), P("head", None), P(None, "head"), P("ctx", "head"),
    )
    return jax.shard_map(
        on_device,
        mesh=mesh,
        in_specs=placed,
        out_specs=(
            P(None, "head"), P("ctx", "head"), P(None, "head"),
            P("ctx", "head"), P("ctx", "head"), P("ctx", "head"),
            P("ctx", "head"), P("ctx", "head"), P("head", "ctx"),
        ),
        check_vma=False,
    )
```

time: 93.3 us -> 65.5 us (0.70)
  Pallas kernels: 82.2 us -> 64.7 us
  local copies, waits for them, and re-layouts: 10.2 us -> 0 us
    pallas_call x1, Pallas kernels: 82.2 us -> 62.3 us  [on_device(): pl.pallas_call(kernel, out_shape=[jax.ShapeDtypeStruct(s, d) for s, d in...]
    unnamed x18 -> x0, local copies, waits for them, and re-layouts: 8.26 us -> none
    pallas_call x0 -> x1, Pallas kernels: none -> 2.4 us  [on_device(): pl.pallas_call(place, out_shape=[jax.ShapeDtypeStruct(s, d) for s, d in p...]
    pallas_call x1 -> x0, local copies, waits for them, and re-layouts: 1.91 us -> none  [on_device(): pl.pallas_call(kernel, out_shape=[jax.ShapeDtypeStruct(s, d) for s, d in...]
where the time goes in v2:
time: 65.5 us; the launch traced here: 65.4 us
  Pallas kernels  64.7 us (99%)
    pallas_call x1, Pallas kernels, on_device(): pl.pallas_call(kernel, out_shape=[jax.ShapeDtypeStruct(s, d) for s, d in...  62.3 us
    pallas_call x1, Pallas kernels, on_device(): pl.pallas_call(place, out_shape=[jax.ShapeDtypeStruct(s, d) for s, d in p...  2.4 us

profile of v2, /device:TPU:1, one launch (start us, length us, event | category | flops | bytes accessed | tf_op | source)
XLA Modules:
  0.0 65.4 jit_solution(15056434157300641073)
XLA Ops:
  0.6 62.3 %shard_map.187 = (bf16[128,384]{1,0:T(8,128)(2,1)}, bf16[128,384]{1,0:T(8,128)(2,1)}, bf16[128,384]{1,0:T(8,128)(2,1)}, bf16[128,384]{1,0:T(8,128)(2,1)}, bf16[3...) custom-call(bf16[512,384]{1,0:T(8,128)(2,1)} %cq.1, ...), custom_call_target="tpu_custom_call" | custom-call | flops 7000000000 | bytes 8000000 | tf_op jit(solution)/shard_map/pallas_call | solution.py:630
  63.0 2.4 %shard_map.188 = (bf16[2,4,2,32,384]{4,3,2,1,0:T(8,128)(2,1)}, bf16[128,384]{1,0:T(8,128)(2,1)}, bf16[2,4,2,32,384]{4,3,2,1,0:T(8,128)(2,1)}, bf16[32,384]{1,0:T...) custom-call(bf16[128,384]{1,0:T(8,128)(2,1)} %get-tuple-element.27.f, ...), custom_call_target="tpu_custom_call" | custom-call | tf_op jit(solution)/shard_map/pallas_call | solution.py:698

commit v3 on v2

--- a/solution.py
+++ b/solution.py
@@ -31,11 +31,11 @@
 
 def kernel(
     cq, ck_in, cv_in, fq, fk, fv, csz, fsz, fpos, w_in, cc, fc,
-    fout_o, fdq_o, fdk_o, fdv_o, cdk_o, cdv_o, wg_o, obuf_o, qbuf_o,
+    fout_o, fdq_o, fdk_o, fdv_o, cdk_o, cdv_o, wg_o, cbuf_o,
     ck, cv, w, q2, qc, kv, cotb, scx, ksc, tbuf, ebuf, ecds, ecx, attn_all, do_c, gcn, gcx, do2,
     on_s, on_r, st_s, st_r, dq_s, dq_r,
     pa, pw, sa, sw, az, wz, wx,
-    oc, ocr, ocx, of, ofr, ofx, obuf, qbuf, wsend, wrecv,
+    oc, ocr, ocx, of, ofr, ofx, cbuf, wsend, wrecv,
     fout, fdq, fdk, fdv, cdk, cdv, wg,
     ssem, rsem, isem, osem,
 ):
@@ -159,8 +159,7 @@
         for h in range(HL)
     ]
     cot_gather = Gather(lambda r, p: cotb.at[r, p], None, y, xl, py, pxl, None)
-    out_gather = Gather(lambda r, p: obuf.at[core, r, p], obuf.at[core], z, xh, pz, px, sib)
-    dq_gather = Gather(lambda r, p: qbuf.at[core, r, p], qbuf.at[core], z, xh, pz, px, sib)
+    coarse_gather = Gather(lambda r, p: cbuf.at[core, r, p], cbuf.at[core], z, xh, pz, px, sib)
 
     pl.semaphore_wait(barrier, len(peers))
 
@@ -311,7 +310,7 @@
         ds = (eb.astype(F32) * ((dp - delta) * (inverse_c[h] * factor))).astype(BF)
         for i in range(2):
             ecds[h, i, 1] = ds[:, HALF * i : HALF * (i + 1)]
-        qbuf[core, z, xh, :, cols_h] = dot(ds, ck[:, cols_h], NN).astype(BF)
+        cbuf[core, z, xh, CR : 2 * CR, cols_h] = dot(ds, ck[:, cols_h], NN).astype(BF)
 
     def backward(h):
         cols_h = slice(h * DH, (h + 1) * DH)
@@ -441,9 +440,46 @@
                 value = value + up(self.from_ring[i])
             return value
 
+    class RingPair:
+        def __init__(self, src, from_sib, from_ring, from_pair):
+            self.src, self.from_sib, self.from_ring, self.from_pair = src, from_sib, from_ring, from_pair
+
+        def a(self):
+            self.cs = send(self.src[0], self.from_sib, sib)
+
+        def b(self):
+            mine = self.src[1]
+            self.cs.wait_recv()
+            self.cr = []
+            for i, r in enumerate(rings):
+                mine[r] = (up(mine[r]) + up(self.from_sib[r])).astype(BF)
+                self.cr.append(send(mine.at[r], self.from_ring.at[i], pz[i]))
+
+        def c(self):
+            mine = self.src[1]
+            for copy in self.cr:
+                copy.wait_recv()
+
+            def total(p):
+                value = up(mine[z, p]) + up(self.from_sib[z, p])
+                for i in range(3):
+                    value = value + up(self.from_ring[i, p])
+                return value
+
+            mine[z, 1 - xh] = total(1 - xh).astype(BF)
+            self.cx = send(mine.at[z, 1 - xh], self.from_pair, px)
+            self.kept = total(xh)
+
+        def d(self):
+            self.cx.wait_recv()
+            return self.kept + up(self.from_pair[...])
+
     sums_a = [RingOnly((pa.at[h, 1 - core], pa.at[h, core]), sa.at[h], az.at[h]) for h in range(HL)]
     sums_w = [
-        PairFirst((pw.at[h, 1 - core], pw.at[h, core]), sw.at[h], wz.at[h], wx.at[h]) for h in range(HL)
+        RingPair((pw.at[h, 1 - core], pw.at[h, core]), sw.at[h], wz.at[h], wx.at[h, 0])
+        if h < 2
+        else PairFirst((pw.at[h, 1 - core], pw.at[h, core]), sw.at[h], wz.at[h, :, 0], wx.at[h])
+        for h in range(HL)
     ]
     coarse_sum = RingFirst(oc, ocr, ocx, (y2, y1, y3), y, xl, py, pxl)
     fine_sum = RingFirst(of, ofr, ofx, (y2, y1, y3), y, xl, py, pxl)
@@ -465,24 +501,22 @@
         cdk[:, cols_h] = total[256:288].astype(BF)
         cdv[:, cols_h] = total[288:320].astype(BF)
 
-    def finish_w():
-        for h in range(HL):
-            total = sums_w[h].d()
-            for i in range(3):
-                piece = total[64 * i : 64 * i + 64]
-                wsend[h, 128 * i : 128 * i + 128, :] = jnp.concatenate([piece, piece], axis=0).T
+    def finish_w(h):
+        total = sums_w[h].d()
+        for i in range(3):
+            piece = total[64 * i : 64 * i + 64]
+            wsend[h, 128 * i : 128 * i + 128, :] = jnp.concatenate([piece, piece], axis=0).T
         other = pl.ds(pl.multiple_of((1 - core) * 192, 64), 192)
-        return send(wsend.at[:, other], wrecv, sib)
-
-    def finish_weight(copy):
+        return send(wsend.at[h, other], wrecv.at[h], sib)
+
+    def finish_weight(h, copy):
         copy.wait_recv()
-        for h in range(HL):
-            mine = wsend[h, pl.ds(pl.multiple_of(core * 192, 64), 192), :]
-            wg[:, h * DH : (h + 1) * DH] = jnp.where((lane < 64) == (core == 0), mine, wrecv[h])
+        mine = wsend[h, pl.ds(pl.multiple_of(core * 192, 64), 192), :]
+        wg[:, h * DH : (h + 1) * DH] = jnp.where((lane < 64) == (core == 0), mine, wrecv[h])
 
     def coarse_done():
-        obuf[core, z, xh] = coarse_sum.d().astype(BF)
-        out_gather.a()
+        cbuf[core, z, xh, 0:CR, :] = coarse_sum.d().astype(BF)
+        coarse_gather.a()
 
     def fine_done():
         fout[...] = fine_sum.d().astype(BF)
@@ -502,11 +536,11 @@
     for h in range(HL):
         coarse_forward(h)
     gather_a(1)
+    cot_gather.b()
+    gather_a(2)
     in_w.wait()
     coarse_project()
     coarse_sum.b()
-    cot_gather.b()
-    gather_a(2)
     g[0].d()
     c_scale.wait_recv()
     row_scale[0] = jnp.concatenate([fsc_col, column(scx[...].astype(F32)[0:1])], axis=0)
@@ -518,14 +552,13 @@
             ksc[:, at : at + 128] = kv[0, planes[i], r, 256:272, :].astype(F32)[0:8]
     x0 = forward(0)
     g[1].d()
-    coarse_sum.c()
     g[1].e()
     x1 = forward(1)
     g[2].d()
+    g[2].e()
+    x2 = forward(2)
     cot_gather.d()
     c_do = grad_attn()
-    g[2].e()
-    x2 = forward(2)
     for h in range(HL):
         coarse_backward(h)
     c_ec = send(ecds.at[:, 1 - xh], ecx, px)
@@ -533,56 +566,56 @@
     combine(0, x0)
     weight_grad(0)
     W[0].a()
-    coarse_done()
-    dq_gather.a()
     combine(1, x1)
     weight_grad(1)
     W[1].a()
+    W[0].b()
+    coarse_sum.c()
     c_do.wait_recv()
     c_ec.wait_recv()
     c_gc.wait_recv()
+    coarse_done()
     run(backward(0), [(1, A[0].a)])
-    W[0].b()
+    W[1].b()
     combine(2, x2)
     weight_grad(2)
     W[2].a()
     A[0].b()
     run(backward(1), [(1, A[1].a)])
-    W[1].b()
+    W[2].b()
+    coarse_gather.b()
     fine_project()
     fine_sum.b()
     A[1].b()
     run(backward(2), [(1, A[2].a)])
-    W[2].b()
     c_dq = send(dq_s, dq_r, px)
+    W[0].c()
     A[2].b()
-    W[0].c()
-    out_gather.b()
-    dq_gather.b()
+    W[1].c()
     finish_a(0)
-    W[1].c()
-    out_gather.d()
-    dq_gather.d()
+    W[2].c()
+    c_w0 = finish_w(0)
     finish_a(1)
-    W[2].c()
+    c_w1 = finish_w(1)
+    coarse_gather.d()
     fine_sum.c()
+    c_dq.wait_recv()
+    for h in range(HL):
+        cols_h = slice(h * DH, (h + 1) * DH)
+        fdq[:, cols_h] = (fdq_own[h] + up(dq_r[:, cols_h])).astype(BF)
+    store(fdq, fdq_o)
     finish_a(2)
     store(fdk, fdk_o)
     store(fdv, fdv_o)
     store(cdk, cdk_o)
     store(cdv, cdv_o)
-    c_dq.wait_recv()
-    for h in range(HL):
-        cols_h = slice(h * DH, (h + 1) * DH)
-        fdq[:, cols_h] = (fdq_own[h] + up(dq_r[:, cols_h])).astype(BF)
-    store(fdq, fdq_o)
-    out_gather.e()
-    store(obuf, obuf_o)
-    dq_gather.e()
-    store(qbuf, qbuf_o)
-    c_w = finish_w()
+    c_w2 = finish_w(2)
+    finish_weight(0, c_w0)
+    finish_weight(1, c_w1)
+    coarse_gather.e()
+    store(cbuf, cbuf_o)
     fine_done()
-    finish_weight(c_w)
+    finish_weight(2, c_w2)
     store(wg, wg_o)
     for copy in started:
         copy.wait_send()
@@ -590,15 +623,15 @@
         copy.wait()
 
 
-def place(fout, fdq, fdk, fdv, cdk, cdv, wg, obuf, qbuf, *rest):
+def place(fout, fdq, fdk, fdv, cdk, cdv, wg, cbuf, *rest):
     outs, held, sem_in, sem_out = rest[:9], rest[9:18], rest[18], rest[19]
     loads = [[] for _ in outs]
     for i, src in ((1, fout), (3, cdk), (4, cdv), (5, fdq), (6, fdk), (7, fdv), (8, wg)):
         loads[i].append((src, held[i]))
     for core in range(2):
         for xh in range(2):
-            loads[0].append((obuf.at[core, :, xh], held[0].at[xh, :, core]))
-            loads[2].append((qbuf.at[core, :, xh], held[2].at[xh, :, core]))
+            loads[0].append((cbuf.at[core, :, xh, pl.ds(0, CR)], held[0].at[xh, :, core]))
+            loads[2].append((cbuf.at[core, :, xh, pl.ds(CR, CR)], held[2].at[xh, :, core]))
     order = (0, 2, 8, 1, 5, 6, 7, 3, 4)
     copies = {}
     count = 0
@@ -624,14 +657,14 @@
     hbm = pl.BlockSpec(memory_space=pl.ANY)
     shapes = [
         ((128, 384), BF), ((128, 384), BF), ((128, 384), BF), ((128, 384), BF), ((32, 384), BF),
-        ((32, 384), BF), ((192, 384), F32), ((2, 4, 2, CR, 384), BF), ((2, 4, 2, CR, 384), BF),
+        ((32, 384), BF), ((192, 384), F32), ((2, 4, 2, 2 * CR, 384), BF),
     ]
     v = pltpu.VMEM
     raw = pl.pallas_call(
         kernel,
         out_shape=[jax.ShapeDtypeStruct(s, d) for s, d in shapes],
         in_specs=[hbm] * 6 + [smem] * 2 + [vmem] + [hbm] * 3,
-        out_specs=[hbm] * 9,
+        out_specs=[hbm] * 8,
         scratch_shapes=[
             v((512, 384), BF),
             v((512, 384), BF),
@@ -662,7 +695,7 @@
             v((HL, 4, CA, DH), BF),
             v((HL, 4, 2, CW, DH), BF),
             v((HL, 3, CA, DH), BF),
-            v((HL, 3, CW, DH), BF),
+            v((HL, 3, 2, CW, DH), BF),
             v((HL, 4, CW, DH), BF),
             v((4, 2, CR, 384), BF),
             v((3, 2, CR, 384), BF),
@@ -670,8 +703,7 @@
             v((4, 2, FR, 384), BF),
             v((3, 2, FR, 384), BF),
             v((FR, 384), BF),
-            v((2, 4, 2, CR, 384), BF),
-            v((2, 4, 2, CR, 384), BF),
+            v((2, 4, 2, 2 * CR, 384), BF),
             v((HL, 384, 128), F32),
             v((HL, 192, 128), F32),
             v((128, 384), BF),
@@ -698,7 +730,7 @@
     outs = pl.pallas_call(
         place,
         out_shape=[jax.ShapeDtypeStruct(s, d) for s, d in placed],
-        in_specs=[hbm] * 9,
+        in_specs=[hbm] * 8,
         out_specs=[hbm] * 9,
         scratch_shapes=[pltpu.VMEM(s, d) for s, d in placed]
         + [pltpu.SemaphoreType.DMA((15,)), pltpu.SemaphoreType.DMA((9,))],

time: 65.5 us -> 61.2 us (0.934)
  Pallas kernels: 64.7 us -> 60.4 us
    pallas_call x1, Pallas kernels: 62.3 us -> 58 us  [on_device(): pl.pallas_call(kernel, out_shape=[jax.ShapeDtypeStruct(s, d) for s, d in...]
where the time goes in v3:
time: 61.2 us; the launch traced here: 61 us
  Pallas kernels  60.4 us (99%)
  between operations  0.65 us (1%)
    pallas_call x1, Pallas kernels, on_device(): pl.pallas_call(kernel, out_shape=[jax.ShapeDtypeStruct(s, d) for s, d in...  58 us
    pallas_call x1, Pallas kernels, on_device(): pl.pallas_call(place, out_shape=[jax.ShapeDtypeStruct(s, d) for s, d in p...  2.4 us

profile of v3, /device:TPU:1, one launch (start us, length us, event | category | flops | bytes accessed | tf_op | source)
XLA Modules:
  0.0 61.0 jit_solution(4456594981888732847)
XLA Ops:
  0.6 58.0 %shard_map.187 = (bf16[128,384]{1,0:T(8,128)(2,1)}, bf16[128,384]{1,0:T(8,128)(2,1)}, bf16[128,384]{1,0:T(8,128)(2,1)}, bf16[128,384]{1,0:T(8,128)(2,1)}, bf16[3...) custom-call(bf16[512,384]{1,0:T(8,128)(2,1)} %cq.1, ...), custom_call_target="tpu_custom_call" | custom-call | flops 7000000000 | bytes 8000000 | tf_op jit(solution)/shard_map/pallas_call | solution.py:663
  58.6 2.4 %shard_map.188 = (bf16[2,4,2,32,384]{4,3,2,1,0:T(8,128)(2,1)}, bf16[128,384]{1,0:T(8,128)(2,1)}, bf16[2,4,2,32,384]{4,3,2,1,0:T(8,128)(2,1)}, bf16[32,384]{1,0:T...) custom-call(bf16[128,384]{1,0:T(8,128)(2,1)} %get-tuple-element.26.f, ...), custom_call_target="tpu_custom_call" | custom-call | tf_op jit(solution)/shard_map/pallas_call | solution.py:730

commit v4 on v3

--- a/solution.py
+++ b/solution.py
@@ -267,14 +267,16 @@
         attn_all[0:FR, cols_h] = both[0:FR]
         attn_all[R : R + FR, cols_h] = both[FR:]
 
-    def grad_attn():
-        acc = jnp.zeros((R, HL * DH), F32)
+    def grad_attn(h):
+        cols_h = slice(h * DH, (h + 1) * DH)
+        acc = jnp.zeros((R, DH), F32)
         for block in range(8):
-            acc = acc + dot(cotb[block % 4, block // 4], w[:, block * 384 : (block + 1) * 384], NT)
+            acc = acc + dot(cotb[block % 4, block // 4], w[cols_h, block * 384 : (block + 1) * 384], NT)
         acc = acc.astype(BF)
-        do2[0:FR, :] = acc[0:FR]
-        do_c[...] = acc[FR:R]
-        return send(do2.at[own_rows], do2.at[pair_rows], px)
+        do2[0:FR, cols_h] = acc[0:FR]
+        do_c[:, cols_h] = acc[FR:R]
+        hs = pl.ds(h * DH, DH)
+        return send(do2.at[own_rows, hs], do2.at[pair_rows, hs], px)
 
     def weight_grad(h):
         a_t = attn_all[0:R, h * DH : (h + 1) * DH].astype(F32).T.astype(BF)
@@ -558,7 +560,7 @@
     g[2].e()
     x2 = forward(2)
     cot_gather.d()
-    c_do = grad_attn()
+    c_do = [grad_attn(h) for h in range(HL)]
     for h in range(HL):
         coarse_backward(h)
     c_ec = send(ecds.at[:, 1 - xh], ecx, px)
@@ -571,7 +573,7 @@
     W[1].a()
     W[0].b()
     coarse_sum.c()
-    c_do.wait_recv()
+    c_do[0].wait_recv()
     c_ec.wait_recv()
     c_gc.wait_recv()
     coarse_done()
@@ -580,16 +582,18 @@
     combine(2, x2)
     weight_grad(2)
     W[2].a()
+    fine_project()
+    fine_sum.b()
     A[0].b()
+    c_do[1].wait_recv()
     run(backward(1), [(1, A[1].a)])
     W[2].b()
     coarse_gather.b()
-    fine_project()
-    fine_sum.b()
     A[1].b()
+    W[0].c()
+    c_do[2].wait_recv()
     run(backward(2), [(1, A[2].a)])
     c_dq = send(dq_s, dq_r, px)
-    W[0].c()
     A[2].b()
     W[1].c()
     finish_a(0)

time: 61.2 us -> 61.4 us (level)
  no operation moved by 1% of the time
where the time goes in v4:
time: 61.4 us; the launch traced here: 61.3 us
  Pallas kernels  60.6 us (99%)
  between operations  0.65 us (1%)
    pallas_call x1, Pallas kernels, on_device(): pl.pallas_call(kernel, out_shape=[jax.ShapeDtypeStruct(s, d) for s, d in...  58.2 us
    pallas_call x1, Pallas kernels, on_device(): pl.pallas_call(place, out_shape=[jax.ShapeDtypeStruct(s, d) for s, d in p...  2.4 us

profile of v4, /device:TPU:1, one launch (start us, length us, event | category | flops | bytes accessed | tf_op | source)
XLA Modules:
  0.0 61.3 jit_solution(14599769665256831072)
XLA Ops:
  0.6 58.2 %shard_map.187 = (bf16[128,384]{1,0:T(8,128)(2,1)}, bf16[128,384]{1,0:T(8,128)(2,1)}, bf16[128,384]{1,0:T(8,128)(2,1)}, bf16[128,384]{1,0:T(8,128)(2,1)}, bf16[3...) custom-call(bf16[512,384]{1,0:T(8,128)(2,1)} %cq.1, ...), custom_call_target="tpu_custom_call" | custom-call | flops 7000000000 | bytes 8000000 | tf_op jit(solution)/shard_map/pallas_call | solution.py:667
  58.9 2.4 %shard_map.188 = (bf16[2,4,2,32,384]{4,3,2,1,0:T(8,128)(2,1)}, bf16[128,384]{1,0:T(8,128)(2,1)}, bf16[2,4,2,32,384]{4,3,2,1,0:T(8,128)(2,1)}, bf16[32,384]{1,0:T...) custom-call(bf16[128,384]{1,0:T(8,128)(2,1)} %get-tuple-element.26.f, ...), custom_call_target="tpu_custom_call" | custom-call | tf_op jit(solution)/shard_map/pallas_call | solution.py:734
